TPU v7x, 32 devices: a whole 2x2x4 slice. The times are simulated.
32 devices in a mesh: page: 8 (over z, x), band: 4 (over y, core).
Axes of the slice: x: 2, y: 2, z: 4, core: 2. Of those that a mesh axis runs over, the one named last changes fastest.
Arguments:
- hidden: bfloat16 [32768, 768], P(('page', 'band')), may hold values from -6 to 6
- page_ids: int32 [32768], P(('page', 'band')), may hold values from 0 to 1, as said below
- key_mask: int32 [32768], P(('page', 'band')), may hold values from 0 to 1, as said below
- out_grad: bfloat16 [32768, 768], P(('page', 'band')), may hold values from -6 to 6
- w_query: bfloat16 [768, 768], replicated, may hold values from -0.4375 to 0.4375
- b_query: float32 [768], replicated, may hold values from -3 to 3
- w_key: bfloat16 [768, 768], replicated, may hold values from -0.21875 to 0.21875
- w_value: bfloat16 [768, 768], replicated, may hold values from -0.21875 to 0.21875
- b_value: float32 [768], replicated, may hold values from -3 to 3
- w_out: bfloat16 [768, 768], replicated, may hold values from -0.875 to 0.875
- b_out: float32 [768], replicated, may hold values from -3 to 3
- gain_one: float32 [768], replicated, may hold values from 0.5 to 1.5
- shift_one: float32 [768], replicated, may hold values from -2 to 2
- w_up: bfloat16 [768, 3072], replicated, may hold values from -0.21875 to 0.21875
- b_up: float32 [3072], replicated, may hold values from -3 to 3
- w_down: bfloat16 [3072, 768], replicated, may hold values from -0.109375 to 0.109375
- b_down: float32 [768], replicated, may hold values from -2 to 2
- gain_two: float32 [768], replicated, may hold values from 0.5 to 1.5
- shift_two: float32 [768], replicated, may hold values from -2 to 2
Outputs:
- output: bfloat16 [32768, 768], P(('page', 'band'))
- input_grad: bfloat16 [32768, 768], P(('page', 'band'))
- grad_w_query: float32 [768, 768], replicated
- grad_b_query: float32 [768], replicated
- grad_w_key: float32 [768, 768], replicated
- grad_w_value: float32 [768, 768], replicated
- grad_b_value: float32 [768], replicated
- grad_w_out: float32 [768, 768], replicated
- grad_b_out: float32 [768], replicated
- grad_gain_one: float32 [768], replicated
- grad_shift_one: float32 [768], replicated
- grad_w_up: float32 [768, 3072], replicated
- grad_b_up: float32 [3072], replicated
- grad_w_down: float32 [3072, 768], replicated
- grad_b_down: float32 [768], replicated
- grad_gain_two: float32 [768], replicated
- grad_shift_two: float32 [768], replicated
Inputs may be any that keep to these rules, and one draw needn't show every extreme that they name: Within each block of 1024 slots the slots with key_mask 1 come first; 32768 // 1024 blocks in all, and some block is full of them in every draw. `page_ids`: document within its document group; within a block the slots with key_mask 1 are in order of document, and every document of the group has such slots in every block of the group.
All inputs are finite; a program needn't handle non-finite values.
Results may differ from a plain program's by a relative error of at most 0.015.
The roundings to bfloat16 on the way count: a program that leaves them out, or rounds other values in their place, can miss the bound.
Values may be sent and summed in bfloat16 or wider, within the bound.
No kernel may reach another device: no remote copies, remote signals or barrier semaphores. Data moves between devices by JAX's collectives and lax.ppermute only.
A program may use at most 256 MiB of HBM per device.

v0:
```python
import functools

import jax
import jax.numpy as jnp
from jax import lax
from jax.experimental import pallas as pl
from jax.experimental.pallas import tpu as pltpu
from jax.sharding import PartitionSpec as P


HEAD = 64
PAIR = 128
BLOCKED = -1e30
SAFE = 60.0
SOME_VMEM = 48 * 2**20
VMEM = 60 * 2**20
NT = (((1,), (1,)), ((), ()))
NN = (((1,), (0,)), ((), ()))
TN = (((0,), (0,)), ((), ()))
F32 = jnp.float32
BF16 = jnp.bfloat16
SCALE = HEAD**-0.5
TILE = 256


def mm(a, b, dims):
    return lax.dot_general(a, b, dims, preferred_element_type=F32)


def col_sum(x):
    return jnp.sum(x, axis=0, keepdims=True)


def tile_at(i, tile=TILE):
    return pl.ds(pl.multiple_of(i * tile, tile), tile)


def parts(x):
    hi = x.astype(BF16)
    rest = x - hi.astype(F32)
    mid = rest.astype(BF16)
    return hi, mid, (rest - mid.astype(F32)).astype(BF16)


def same_half():
    a, b = (lax.broadcasted_iota(jnp.int32, (PAIR, PAIR), i) < HEAD for i in (0, 1))
    return jnp.where(a == b, 1.0, 0.0).astype(BF16)


def left_lanes():
    return lax.broadcasted_iota(jnp.int32, (1, PAIR), 1) < HEAD


def together(bands, whole):
    rows = bands[0].shape[0]
    for i, band in enumerate(bands):
        whole[i * rows:(i + 1) * rows, :] = band[...]


def attend_kernel(tiles, q_ref, k_own, k_mate, k_far, v_own, v_mate, v_far, qtag_ref, ktag_ref, o_ref, ext_ref,
                  kx, qx0, qx1, vt, acc0, acc1, top0, top1):
    rows, near = q_ref.shape[0], ktag_ref.shape[0]
    left = left_lanes()
    q_pair = q_ref[...] * jnp.asarray(SCALE, BF16)
    zero = jnp.zeros_like(q_pair)
    qx0[:, :PAIR] = jnp.where(left, q_pair, zero)
    qx1[:, :PAIR] = jnp.where(left, zero, q_pair)
    qx0[:, PAIR:] = qtag_ref[...]
    qx1[:, PAIR:] = qtag_ref[...]
    kx[:, PAIR:] = ktag_ref[...]
    vt[HEAD:PAIR, :] = jnp.ones((HEAD, near), BF16)
    halves = same_half()

    def longest(x):
        x = x.astype(F32)
        return jnp.max(mm((x * x).astype(BF16), halves, NN), axis=0, keepdims=True)

    reach = 0.0
    for i, (k_band, v_band) in enumerate(((k_own, v_own), (k_mate, v_mate), (k_far, v_far))):
        span = slice(i * rows, (i + 1) * rows)
        kx[span, :PAIR] = k_band[...]
        turned = v_band[...].T
        vt[:HEAD, span] = turned[:HEAD]
        vt[PAIR:, span] = turned[HEAD:]
        reach = jnp.maximum(reach, longest(k_band[...]))
    plain = jnp.max(reach * longest(q_pair)) < (SAFE * 0.98) ** 2
    heads = ((acc0, top0, qx0, slice(0, PAIR)), (acc1, top1, qx1, slice(HEAD, HEAD + PAIR)))
    for acc, *_ in heads:
        acc[...] = jnp.zeros_like(acc)

    @pl.when(plain)
    def _():
        for _, top, *_ in heads:
            top[...] = jnp.zeros_like(top)

        def per_band(band, _):
            for n in range(1, rows // TILE + 1):
                @pl.when(tiles[band] == n)
                def _():
                    ks = pl.ds(pl.multiple_of(band * rows, rows), n * TILE)
                    scores = [mm(kx[ks, :], qx[...], NT) for _, _, qx, _ in heads]
                    probs = [jnp.exp(s).astype(BF16) for s in scores]
                    for (acc, _, _, at), p in zip(heads, probs):
                        acc[...] += mm(vt[at, ks], p, NN)
            return 0

        lax.fori_loop(0, near // rows, per_band, 0)

    @pl.when(jnp.logical_not(plain))
    def _():
        for _, top, *_ in heads:
            top[...] = jnp.full_like(top, -3e38)

        def per_k(ki, _):
            @pl.when(lax.rem(ki, rows // TILE) < tiles[lax.div(ki, rows // TILE)])
            def _():
                ks = tile_at(ki)
                for acc, top, qx, at in heads:
                    s = mm(kx[ks, :], qx[...], NT)
                    old = top[...]
                    new = jnp.maximum(old, jnp.max(s, axis=0, keepdims=True))
                    p = jnp.exp(s - new[:1, :]).astype(BF16)
                    acc[...] = acc[...] * jnp.exp(old - new)[:1, :] + mm(vt[at, ks], p, NN)
                    top[...] = new
            return 0

        lax.fori_loop(0, near // TILE, per_k, 0)

    def finish(qi, _):
        qs = tile_at(qi)
        tags = qtag_ref[qs, :].astype(F32).T[:8]
        place = lax.broadcasted_iota(jnp.int32, (8, TILE), 0)
        out, ext = [], []
        for acc, top, _, at in heads:
            total, plain_out = (acc[HEAD:, qs], acc[:HEAD, qs]) if at.start == 0 else (acc[:HEAD, qs], acc[HEAD:, qs])
            out.append(plain_out / total)
            hi, mid, lo = (x.astype(F32) for x in parts(jnp.log(total[:8]) + top[:, qs]))
            head = jnp.where(place == 2, hi, jnp.where(place == 3, mid, jnp.where(place == 4, lo, tags)))
            ext += [head, jnp.zeros((HEAD - 8, TILE), F32)]
        o_ref[qs, :] = jnp.concatenate(out, axis=0).T.astype(BF16)
        ext_ref[qs, :] = jnp.concatenate(ext, axis=0).T.astype(BF16)
        return 0

    lax.fori_loop(0, rows // TILE, finish, 0)


def attend(q, k, v, qtag, ktag, tiles):
    rows, d = q.shape
    near = len(k) * rows
    part = lambda n: pl.BlockSpec((n, PAIR), lambda p, *_: (0, p))
    fixed = lambda n: pl.BlockSpec((n, PAIR), lambda p, *_: (0, 0))
    return pl.pallas_call(
        attend_kernel,
        grid_spec=pltpu.PrefetchScalarGridSpec(
            num_scalar_prefetch=1,
            grid=(d // PAIR,),
            in_specs=[part(rows)] + [part(rows)] * 6 + [fixed(rows), fixed(near)],
            out_specs=[part(rows)] * 2,
            scratch_shapes=[pltpu.VMEM((n, 2 * PAIR), BF16) for n in (near, rows, rows)] + [pltpu.VMEM((PAIR + HEAD, near), BF16)]
            + [pltpu.VMEM((PAIR, rows), F32)] * 2 + [pltpu.VMEM((8, rows), F32)] * 2,
        ),
        out_shape=[jax.ShapeDtypeStruct((rows, d), BF16)] * 2,
        compiler_params=pltpu.CompilerParams(vmem_limit_bytes=VMEM),
        cost_estimate=pl.CostEstimate(flops=40 * 10**9, bytes_accessed=16 * 2**20, transcendentals=0),
        name="attend",
    )(tiles, q, *k, *v, qtag, ktag)


def hull(qbits, want, nq):
    first, last = jnp.int32(nq), jnp.int32(0)
    for qi in reversed(range(nq)):
        hit = (qbits[qi] & want) != 0
        last = jnp.where(hit & (last == 0), qi + 1, last)
        first = jnp.where(hit, qi, first)
    return first, jnp.maximum(last - first, 0)


def attend_back_kernel(tk, qbits, kbits, q_ref, k_own, k_mate, k_far, v_own, v_mate, v_far, g_ref, o_ref, ext_ref, ktag_ref,
                       own_in, mate_in, far_in, sums_in, *refs):
    (sums, dq_ref, dk_ref, dv_ref, w_ref, k_ref, v_ref, qx0, qx1, gx0, gx1, qt, gt, dq_acc, dk_acc, dv_acc, own_ref, mate_ref,
     far_ref, arrived) = refs[-20:]
    rows, near = q_ref.shape[0], k_ref.shape[0]
    first = pl.program_id(0) == 0
    copies = [pltpu.make_async_copy(a, b, arrived.at[i])
              for i, (a, b) in enumerate(((own_in, own_ref), (mate_in, mate_ref), (far_in, far_ref)))]

    @pl.when(first)
    def _():
        for copy in copies:
            copy.start()

    together((k_own, k_mate, k_far), k_ref)
    together((v_own, v_mate, v_far), v_ref)
    nq = rows // TILE
    left = left_lanes()
    place = lax.broadcasted_iota(jnp.int32, (1, PAIR), 1) % HEAD
    halves = same_half()

    def per_q(qi, _):
        qs = tile_at(qi)
        q_pair, g_pair, ext = q_ref[qs, :], g_ref[qs, :], ext_ref[qs, :]
        qt[:, qs] = q_pair.T
        gt[:, qs] = g_pair.T
        zero = jnp.zeros_like(q_pair)
        hi, mid, _ = parts(g_pair.astype(F32) * o_ref[qs, :].astype(F32))
        hi, mid, _ = parts(mm(hi, halves, NN) + mm(mid, halves, NN))
        inner = jnp.where(place == 2, hi, jnp.where(place == 3, mid, zero))
        scaled = q_pair * jnp.asarray(SCALE, BF16)
        for x0, x1, base, more in ((qx0, qx1, scaled, ext), (gx0, gx1, g_pair, inner)):
            x0[qs, :PAIR] = jnp.where(left, base, zero)
            x1[qs, :PAIR] = jnp.where(left, zero, base)
            x0[qs, PAIR:] = jnp.where(left, more, zero)
            x1[qs, PAIR:] = jnp.where(left, zero, more)
        return 0

    lax.fori_loop(0, nq, per_q, 0)
    dq_acc[...] = jnp.zeros_like(dq_acc)

    def per_k(ki, _):
        first, count = hull(qbits, kbits[ki], nq)
        ks = tile_at(ki, tk)

        @pl.when(count == 0)
        def _():
            dk_acc[:, ks] = jnp.zeros((PAIR, tk), F32)
            dv_acc[:, ks] = jnp.zeros((PAIR, tk), F32)

        for n in range(1, nq + 1):
            @pl.when(count == n)
            def _():
                qs = pl.ds(pl.multiple_of(first * TILE, TILE), n * TILE)
                k_pair, tags = k_ref[ks, :], ktag_ref[ks, :]
                zero = jnp.zeros_like(k_pair)
                kx = jnp.concatenate([k_pair, tags], axis=1)
                vx = jnp.concatenate([v_ref[ks, :], tags], axis=1)
                s0 = mm(qx0[qs, :], kx, NT)
                d0 = mm(gx0[qs, :], vx, NT)
                p0 = jnp.exp(s0)
                s1 = mm(qx1[qs, :], kx, NT)
                ds0 = (p0 * d0).astype(BF16)
                p0 = p0.astype(BF16)
                d1 = mm(gx1[qs, :], vx, NT)
                p1 = jnp.exp(s1)
                dv_acc[:HEAD, ks] = mm(gt[:HEAD, qs], p0, NN)
                dk_acc[:HEAD, ks] = mm(qt[:HEAD, qs], ds0, NN)
                ds1 = (p1 * d1).astype(BF16)
                p1 = p1.astype(BF16)
                dq = mm(ds0, jnp.where(left, k_pair, zero), NN)
                dv_acc[HEAD:, ks] = mm(gt[HEAD:, qs], p1, NN)
                dk_acc[HEAD:, ks] = mm(qt[HEAD:, qs], ds1, NN)
                dq = dq + mm(ds1, jnp.where(left, zero, k_pair), NN)
                dq_acc[qs, :] += dq
        return 0

    lax.fori_loop(0, near // tk, per_k, 0)
    dq = (dq_acc[...] * SCALE).astype(BF16)
    dk = (dk_acc[...] * SCALE).astype(BF16)
    dv = dv_acc[...].astype(BF16)
    dq_ref[...] = dq
    dk_ref[...] = dk.T
    dv_ref[...] = dv.T

    @pl.when(first)
    def _():
        for copy in copies:
            copy.wait()

    w_ref[:, :PAIR] = mm(dq, own_ref[...], TN).T.astype(BF16)
    for i, x in ((1, dk), (2, dv)):
        total = mm(x[:, :rows], own_ref[...], NN)
        total = total + mm(x[:, rows:2 * rows], mate_ref[...], NN)
        total = total + mm(x[:, 2 * rows:], far_ref[...], NN)
        w_ref[:, i * PAIR:(i + 1) * PAIR] = total.T.astype(BF16)
    row = lax.broadcasted_iota(jnp.int32, (8, PAIR), 0)
    by_column = lambda ref: mm(jnp.ones((8, ref.shape[0]), BF16), ref[...], NN)
    sums[...] = jnp.where(row == 4, by_column(dq_ref), jnp.where(row == 5, by_column(dv_ref), sums_in[...]))


def attend_back(pair, pairs, kept, after, q, k, v, g, o, ext, ktag, inputs, qbits, kbits, tk):
    rows, d = q.shape
    near = len(k) * rows
    part = lambda n: pl.BlockSpec((n, PAIR), lambda p, *_: (0, pair + p))
    once = lambda n, m: pl.BlockSpec((n, m), lambda p, *_: (0, 0), pipeline_mode=pl.Buffered(1))
    sums = pl.BlockSpec((8, PAIR), lambda p, *_: (1, pair + p))
    hold = pl.BlockSpec(memory_space=pl.ANY)
    return pl.pallas_call(
        functools.partial(attend_back_kernel, tk),
        grid_spec=pltpu.PrefetchScalarGridSpec(
            num_scalar_prefetch=2,
            grid=(pairs,),
            in_specs=[part(rows)] * 10 + [once(near, PAIR)] + [hold] * 3 + [sums]
            + [hold] * (len(kept) - 1 + len(after)),
            out_specs=[sums, part(rows), part(near), part(near), pl.BlockSpec((d, 3 * PAIR), lambda p, *_: (0, p))],
            scratch_shapes=[pltpu.VMEM((near, PAIR), BF16)] * 2 + [pltpu.VMEM((rows, 2 * PAIR), BF16)] * 4
            + [pltpu.VMEM((PAIR, rows), BF16)] * 2 + [pltpu.VMEM((rows, PAIR), F32)] + [pltpu.VMEM((PAIR, near), F32)] * 2
            + [pltpu.VMEM((rows, d), BF16)] * 3 + [pltpu.SemaphoreType.DMA((3,))],
        ),
        out_shape=[jax.ShapeDtypeStruct((16, d), F32)] + [jax.ShapeDtypeStruct((n, d), BF16) for n in (rows, near, near)]
        + [jax.ShapeDtypeStruct((d, pairs * 3 * PAIR), BF16)],
        input_output_aliases={16 + i: i for i in range(len(kept))},
        compiler_params=pltpu.CompilerParams(vmem_limit_bytes=SOME_VMEM),
        cost_estimate=pl.CostEstimate(flops=18 * pairs * 10**9, bytes_accessed=8 * 2**20, transcendentals=0),
        name="attend_back",
    )(qbits, kbits, q, *k, *v, g, o, ext, ktag, *inputs, *kept, *after)


def project_kernel(x, w_key, w_value, b_value, *refs):
    k_ref, v_ref = refs[-2:]
    k_ref[...] = mm(x[...], w_key[...], NN).astype(BF16)
    v_ref[...] = (mm(x[...], w_value[...], NN) + b_value[...].reshape(1, -1)).astype(BF16)
    if len(refs) > 2:
        w_query, b_query, q_ref = refs[:3]
        q_ref[...] = (mm(x[...], w_query[...], NN) + b_query[...].reshape(1, -1)).astype(BF16)


def project(x, w_key, w_value, b_value, *query):
    rows, d = x.shape
    tr = rows // 2
    tile = pl.BlockSpec((tr, d), lambda i: (i, 0))
    whole = pl.BlockSpec((d, d), lambda i: (0, 0), pipeline_mode=pl.Buffered(1))
    flat = pl.BlockSpec((d,), lambda i: (0,))
    outs = 3 if query else 2
    return pl.pallas_call(
        project_kernel,
        grid=(rows // tr,),
        in_specs=[tile, whole, whole, flat] + [whole, flat] * (outs - 2),
        out_specs=[tile] * outs,
        out_shape=[jax.ShapeDtypeStruct((rows, d), BF16)] * outs,
        compiler_params=pltpu.CompilerParams(vmem_limit_bytes=VMEM),
        cost_estimate=pl.CostEstimate(flops=6 * rows * d * d, bytes_accessed=10 * rows * d, transcendentals=0),
        name="project",
    )(x, w_key, w_value, b_value, *query)


def row_norm(values):
    centred = values - jnp.mean(values, axis=-1, keepdims=True)
    rstd = lax.rsqrt(jnp.mean(centred * centred, axis=-1, keepdims=True) + 1e-12)
    return centred * rstd, rstd


def norm_back(cot, gain, normed, rstd):
    e = cot * gain
    return rstd * (e - jnp.mean(e, axis=-1, keepdims=True) - normed * jnp.mean(e * normed, axis=-1, keepdims=True))


def dense_kernel(tf, hidden, mixed, out_grad, mask, w_out, w_up, w_down, b_out, gain_one, shift_one, b_up, b_down,
                 gain_two, shift_two, result, low_t, mixed_t, d_branch_t, active, d_upper, d_one, d_att, d_mixed, sums, slope,
                 sum_up):
    ff = w_up.shape[1]

    @pl.when(pl.program_id(0) == 0)
    def _():
        sums[...] = jnp.zeros_like(sums)
        sum_up[...] = jnp.zeros_like(sum_up)

    vec = lambda ref: ref[...].reshape(1, -1)
    r1 = hidden[...].astype(F32) + (mm(mixed[...], w_out[...], NN) + vec(b_out))
    n1, s1 = row_norm(r1)
    normed_one = n1 * vec(gain_one) + vec(shift_one)
    low = normed_one.astype(BF16)
    low_t[...] = low.T
    mixed_t[...] = mixed[...].T
    branch = jnp.zeros_like(r1)
    bias = vec(b_up)
    for t in range(0, ff, tf):
        c = pl.ds(t, tf)
        u = mm(low, w_up[:, c], NN) + bias[:, t:t + tf]
        phi = 0.5 + 0.5 * lax.erf(u * (0.5**0.5))
        a = (u * phi).astype(BF16)
        active[:, c] = a
        slope[:, c] = phi + u * (jnp.exp(u * u * -0.5) * 0.3989422804014327)
        branch = branch + mm(a, w_down[c, :], NN)
    n2, s2 = row_norm(normed_one + (branch + vec(b_down)))
    result[...] = (n2 * vec(gain_two) + vec(shift_two)).astype(BF16)
    cot = out_grad[...].astype(F32) * mask[...]
    d_two = norm_back(cot, vec(gain_two), n2, s2)
    db = d_two.astype(BF16)
    d_branch_t[...] = db.T
    sums[0:1, :] += col_sum(cot * n2)
    sums[1:2, :] += col_sum(cot)
    sums[2:3, :] += col_sum(db.astype(F32))
    d_normed = d_two
    for t in range(0, ff, tf):
        c = pl.ds(t, tf)
        du = (mm(db, w_down[c, :], NT) * slope[:, c]).astype(BF16)
        d_upper[:, c] = du
        sum_up[:, c] += col_sum(du.astype(F32))
        d_normed = d_normed + mm(du, w_up[:, c], NT)
    sums[3:4, :] += col_sum(d_normed * n1)
    sums[4:5, :] += col_sum(d_normed)
    d1 = norm_back(d_normed, vec(gain_one), n1, s1)
    d_one[...] = d1
    da = d1.astype(BF16)
    d_att[...] = da
    sums[5:6, :] += col_sum(da.astype(F32))
    d_mixed[...] = mm(da, w_out[...], NT).astype(BF16)

    @pl.when(pl.program_id(0) == pl.num_programs(0) - 1)
    def _():
        d = hidden.shape[1]
        for i in range(ff // d):
            sums[8 + i:9 + i, :] = sum_up[:, i * d:(i + 1) * d]


def dense(hidden, mixed, out_grad, mask, w_out, w_up, w_down, b_out, gain_one, shift_one, b_up, b_down, gain_two,
          shift_two, tr=256, tf=768):
    rows, d = hidden.shape
    ff = w_up.shape[1]
    row = lambda n: pl.BlockSpec((tr, n), lambda i: (i, 0))
    whole = lambda a, b: pl.BlockSpec((a, b), lambda i: (0, 0), pipeline_mode=pl.Buffered(1))
    flat = lambda n: pl.BlockSpec((n,), lambda i: (0,))
    shape = jax.ShapeDtypeStruct
    low = shape((rows, d), BF16)
    return pl.pallas_call(
        functools.partial(dense_kernel, tf),
        grid=(rows // tr,),
        in_specs=[row(d), row(d), row(d), row(1), whole(d, d), whole(d, ff), whole(ff, d), flat(d), flat(d), flat(d),
                  flat(ff), flat(d), flat(d), flat(d)],
        out_specs=[row(d)] + [pl.BlockSpec((d, tr), lambda i: (0, i))] * 3 + [row(ff), row(ff), row(d), row(d), row(d),
                   pl.BlockSpec((16, d), lambda i: (0, 0))],
        out_shape=[low] + [shape((d, rows), BF16)] * 3 + [shape((rows, ff), BF16)] * 2 + [shape((rows, d), F32), low, low,
                   shape((16, d), F32)],
        scratch_shapes=[pltpu.VMEM((tr, ff), F32), pltpu.VMEM((1, ff), F32)],
        compiler_params=pltpu.CompilerParams(vmem_limit_bytes=VMEM),
        cost_estimate=pl.CostEstimate(flops=40 * 10**9, bytes_accessed=40 * 2**20, transcendentals=0),
        name="dense",
    )(hidden, mixed, out_grad, mask.astype(F32).reshape(-1, 1), w_out, w_up, w_down, b_out, gain_one, shift_one, b_up,
      b_down, gain_two, shift_two)


def back_kernel(dk, dv, w_key, w_value, *refs):
    total = mm(dk[...], w_key[...], NT) + mm(dv[...], w_value[...], NT)
    if len(refs) > 1:
        dq, w_query, d_one, mate_part, far_part = refs[:5]
        total = total + mm(dq[...], w_query[...], NT) + d_one[...]
        total = total + mate_part[...].astype(F32) + far_part[...].astype(F32)
    refs[-1][...] = total.astype(BF16)


def back_product(band, dk, dv, w_key, w_value, own=()):
    d = w_key.shape[0]
    rows = dk.shape[0] // 3
    tr = rows // 2
    at = lambda i: (band * (rows // tr) + i, 0)
    row = lambda place: pl.BlockSpec((tr, d), place)
    whole = pl.BlockSpec((d, d), lambda i: (0, 0), pipeline_mode=pl.Buffered(1))
    first = lambda i: (i, 0)
    return pl.pallas_call(
        back_kernel,
        grid=(rows // tr,),
        in_specs=[row(at), row(at), whole, whole] + ([row(first), whole] + [row(first)] * 3 if own else []),
        out_specs=row(first),
        out_shape=jax.ShapeDtypeStruct((rows, d), BF16),
        compiler_params=pltpu.CompilerParams(vmem_limit_bytes=VMEM),
        cost_estimate=pl.CostEstimate(flops=(6 if own else 4) * rows * d * d, bytes_accessed=10 * rows * d, transcendentals=0),
        name="back_product",
    )(dk, dv, w_key, w_value, *own)


ALL = ("page", "band")


def everyone():
    return lax.axis_size("page") * lax.axis_size("band")


def swapped(block, mask):
    return lax.ppermute(block, ALL, [(i, i ^ mask) for i in range(everyone())])


def side(bit):
    return lax.rem(lax.div(lax.axis_index(ALL), bit), 2)


def masks_of(bits):
    masks = [0]
    for bit in reversed(bits):
        masks = masks + [mask | bit for mask in masks]
    return masks


def place_of(bits):
    at = 0
    for bit in bits:
        at = 2 * at + side(bit)
    return at


def dealt(block, bits, axis):
    masks = masks_of(bits)
    size = block.shape[axis] // len(masks)
    place = place_of(bits)
    return [lax.dynamic_slice_in_dim(block, jnp.bitwise_xor(place, i) * size, size, axis) for i in range(len(masks))]


def sent(parts, bits):
    return [swapped(part, mask) for part, mask in zip(parts, masks_of(bits)[1:])]


def summed(parts):
    parts = [part.astype(F32) for part in parts]
    while len(parts) > 1:
        parts = [parts[i] + parts[i + 1] for i in range(0, len(parts), 2)]
    return parts[0].astype(BF16)


class Summing:
    def __init__(self, parts, stages):
        self.stages, self.at = stages, 0
        self.parts = parts

    def advance(self, held=None):
        if self.at < len(self.stages):
            theirs = sent(self.parts[1:], self.stages[self.at])
            if held is not None:
                theirs, held = lax.optimization_barrier((theirs, held))
            block = summed([self.parts[0]] + theirs)
            self.at += 1
            self.parts = dealt(block, self.stages[self.at], 0) if self.at < len(self.stages) else [block]
        return held


def in_order(parts, bits):
    for i, bit in enumerate(bits):
        far = 1 << (len(bits) - 1 - i)
        flip = side(bit) == 1
        parts = [jnp.where(flip, parts[j ^ far], parts[j]) for j in range(len(parts))]
    return jnp.concatenate(parts)


def products_kernel(low, mixed, d_branch, d_upper, d_att, active, made):
    step = pl.program_id(0)
    count = (pl.num_programs(0) - 1) // 2
    middle = (step >= count) & (step < 2 * count)
    for here, left, right in ((step < count, d_branch, active), (middle, low, d_upper), (step == 2 * count, mixed, d_att)):
        @pl.when(here)
        def _():
            made[...] = mm(left[...], right[...], NN).astype(BF16)


def feed_forward_products(low, mixed, d_branch, d_upper, d_att, active):
    d, rows = low.shape
    count = active.shape[1] // d
    once = lambda n, m: pl.BlockSpec((n, m), lambda j: (0, 0), pipeline_mode=pl.Buffered(1))
    along = lambda first: pl.BlockSpec((rows, d), lambda j: (0, jnp.clip(j - first, 0, count - 1)))
    return pl.pallas_call(
        products_kernel,
        grid=(2 * count + 1,),
        in_specs=[once(d, rows)] * 3 + [along(count), once(rows, d), along(0)],
        out_specs=pl.BlockSpec((d, d), lambda j: (0, j)),
        out_shape=jax.ShapeDtypeStruct((d, (2 * count + 1) * d), BF16),
        compiler_params=pltpu.CompilerParams(vmem_limit_bytes=VMEM),
        cost_estimate=pl.CostEstimate(flops=2 * rows * d * d * (2 * count + 1), bytes_accessed=20 * d * d * count,
                                      transcendentals=0),
        name="products",
    )(low, mixed, d_branch, d_upper, d_att, active)


def place_kernel(from_down, from_up, from_out, down, up, out):
    down[...] = from_down[...].T.astype(F32)
    up[...] = from_up[...].astype(F32)
    out[...] = from_out[...].astype(F32)


def feed_forward_whole(got):
    d = got.shape[0]
    ff = (got.shape[1] - d) // 2
    steps = d // PAIR
    row = lambda n: pl.BlockSpec((PAIR, n), lambda j: (j, 0))
    return pl.pallas_call(
        place_kernel,
        grid=(steps,),
        in_specs=[pl.BlockSpec((d, ff // steps), lambda j: (0, j)), pl.BlockSpec((PAIR, ff), lambda j: (j, 1)),
                  pl.BlockSpec((PAIR, d), lambda j: (j, 2 * ff // d))],
        out_specs=[pl.BlockSpec((ff // steps, d), lambda j: (j, 0)), row(ff), row(d)],
        out_shape=[jax.ShapeDtypeStruct(shape, F32) for shape in ((ff, d), (d, ff), (d, d))],
        compiler_params=pltpu.CompilerParams(vmem_limit_bytes=VMEM),
        cost_estimate=pl.CostEstimate(flops=0, bytes_accessed=12 * ff * d, transcendentals=0),
        name="place",
    )(got, got, got)


def split_kernel(x, q, k, v):
    for i, out in enumerate((q, k, v)):
        for p in range(q.shape[1] // PAIR):
            at = (3 * p + i) * PAIR
            out[:, p * PAIR:(p + 1) * PAIR] = x[:, at:at + PAIR].astype(F32)


def split_projections(x):
    d = x.shape[0]
    tr = d // 3
    row = lambda n: pl.BlockSpec((tr, n), lambda i: (i, 0))
    return pl.pallas_call(
        split_kernel,
        grid=(3,),
        in_specs=[row(3 * d)],
        out_specs=[row(d)] * 3,
        out_shape=[jax.ShapeDtypeStruct((d, d), F32)] * 3,
        compiler_params=pltpu.CompilerParams(vmem_limit_bytes=32 * 2**20),
        cost_estimate=pl.CostEstimate(flops=0, bytes_accessed=18 * d * d, transcendentals=0),
        name="split",
    )(x)


def tag_columns(page_ids, near_tags):
    place = jnp.arange(PAIR)[None, :] % HEAD
    qtag = jnp.where(jnp.arange(PAIR)[None, :] == page_ids[:, None], 1.0, 0.0).astype(BF16)
    ktag = jnp.where((place < 2) & (near_tags[:, None] != place + 1), BLOCKED, 0.0)
    return qtag, jnp.where((place >= 2) & (place < 5), -1.0, ktag).astype(BF16)


def tokens_of(near_tags, rows):
    have = jnp.sum((near_tags.reshape(-1, rows) > 0).astype(jnp.int32), axis=1)
    return (have + (TILE - 1)) // TILE


def tile_bits(tags, tile):
    tags = tags.reshape(-1, tile)
    return sum(jnp.max(jnp.where(tags == d + 1, 1 << d, 0), axis=1) for d in range(2)).astype(jnp.int32)


def body(hidden, page_ids, key_mask, out_grad, w_query, b_query, w_key, w_value, b_value, w_out, b_out, gain_one,
         shift_one, w_up, b_up, w_down, b_down, gain_two, shift_two):
    rows, d = hidden.shape
    bands = lax.axis_size("band")
    mates = [(i, i ^ 1) for i in range(bands)]
    across = [(i, i + 1) for i in range(1, bands - 1, 2)] + [(i + 1, i) for i in range(1, bands - 1, 2)]
    to_mate = lambda x: lax.ppermute(x, "band", mates)
    to_across = lambda x: lax.ppermute(x, "band", across)

    key_tags = jnp.where(key_mask == 1, page_ids + 1, 0)
    far, mate = to_across(hidden), to_mate(hidden)
    near_tags = jnp.concatenate([key_tags, to_mate(key_tags), to_across(key_tags)])
    queries, *own_pair = project(hidden, w_key, w_value, b_value, w_query, b_query)
    mate_pair, far_pair = project(mate, w_key, w_value, b_value), project(far, w_key, w_value, b_value)
    keys, values = zip(own_pair, mate_pair, far_pair)
    qtag, ktag = tag_columns(page_ids, near_tags)
    tk = 512
    tokens, qbits, kbits = tokens_of(near_tags, rows), tile_bits(key_tags, TILE), tile_bits(near_tags, tk)
    tokens, qbits, kbits, queries = lax.optimization_barrier((tokens, qbits, kbits, queries))

    mixed, ext = attend(queries, keys, values, qtag, ktag, tokens)
    (result, low_t, mixed_t, d_branch_t, active, d_upper, d_one, d_att, d_mixed, sums) = dense(
        hidden, mixed, out_grad, key_mask, w_out, w_up, w_down, b_out, gain_one, shift_one, b_up, b_down, gain_two,
        shift_two)

    count = everyone().bit_length() - 1
    core, y, x, z = 1, 2, bands, 2 * bands
    rest = [1 << i for i in range(count) if 1 << i not in (core, y, x, z)]
    direct = [[core], [x, y]] + [([z] + rest)[i:i + 2] for i in range(0, 1 + len(rest), 2)]

    products = feed_forward_products(low_t, mixed_t, d_branch_t, d_upper, d_att, active)
    products, d_mixed = lax.optimization_barrier((products, d_mixed))
    shares = lax.psum_scatter(products, ALL, scatter_dimension=0, tiled=True)

    pairs = d // PAIR
    kept, made, at, after = (sums,), [], 0, []
    for size in (2, 2, pairs - 4):
        *kept, made_now = attend_back(at, size, kept, after, queries, keys, values, d_mixed, mixed, ext, ktag,
                                      (hidden, mate, far), qbits, kbits, tk)
        at += size
        made.append(made_now)
        if at == 2:
            early = Summing(dealt(made[0], [core], 0), direct[:2])
            after = early.parts
        elif at == 4:
            kept[1] = early.advance(kept[1])
            late = Summing(dealt(made[1], [core], 0), direct[:1])
            after = early.parts + late.parts
    for stream in (early, late):
        kept[1] = stream.advance(kept[1])
    vectors, dq, dk, dv = kept

    keep, send = dealt(made[-1], [core], 0)
    vectors = vectors.astype(BF16)
    dk, send = lax.optimization_barrier((dk, send))
    theirs = [swapped(send, core), swapped(vectors, core)]
    far_part = back_product(2, dk, dv, w_key, w_value)
    theirs, far_part = lax.optimization_barrier((theirs, far_part))
    far_part = to_across(far_part)
    block = jnp.concatenate([late.parts[0], summed([keep, theirs[0]])], axis=1)
    vectors = summed([vectors, theirs[1]])
    vectors = jnp.concatenate([vectors[:8], vectors[8:]], axis=1)
    for i, bits in enumerate(direct[1:]):
        parts = dealt(block, bits, 0)
        send = [jnp.concatenate([part, vectors]) for part in parts[1:]]
        if i == 0:
            send, dk = lax.optimization_barrier((send, dk))
        theirs = sent(send, bits)
        if i == 0:
            shares, dk = lax.optimization_barrier((shares, dk))
            got = lax.all_gather(shares, ALL, axis=0, tiled=True)
            mate_part = back_product(1, dk, dv, w_key, w_value)
            theirs, mate_part = lax.optimization_barrier((theirs, mate_part))
            mate_part = to_mate(mate_part)
        elif i == 1:
            input_grad = back_product(0, dk, dv, w_key, w_value, (dq, w_query, d_one, mate_part, far_part))
            theirs, input_grad = lax.optimization_barrier((theirs, input_grad))
        size = parts[0].shape[0]
        block = summed([parts[0]] + [other[:size] for other in theirs])
        vectors = summed([vectors] + [other[size:] for other in theirs])
        if i == 0:
            block = jnp.concatenate([early.parts[0], block], axis=1)
            vectors = jnp.pad(vectors, ((0, 0), (0, block.shape[1] - vectors.shape[1])))
    vectors = jnp.concatenate([vectors[:, :d], vectors[:, d:2 * d]]).astype(F32)

    for bits in reversed(direct):
        theirs = sent([block] * (len(masks_of(bits)) - 1), bits)
        block = in_order([block] + theirs, bits)
    grad_query, grad_key, grad_value = split_projections(block)
    got, grad_query = lax.optimization_barrier((got, grad_query))
    grad_down, grad_up, grad_out = feed_forward_whole(got)
    return (
        result,
        input_grad,
        grad_query,
        vectors[12],
        grad_key,
        grad_value,
        vectors[13],
        grad_out,
        vectors[5],
        vectors[3],
        vectors[4],
        grad_up,
        vectors[8:12].reshape(-1),
        grad_down,
        vectors[2],
        vectors[0],
        vectors[1],
    )


def solution(mesh):
    split = P(("page", "band"), None)
    line = P(("page", "band"))
    return jax.shard_map(
        body,
        mesh=mesh,
        in_specs=(split, line, line, split) + (P(),) * 15,
        out_specs=(split, split) + (P(),) * 15,
        check_vma=False,
    )
```

profile of v0, /device:TPU:0, one launch (start us, length us, event | category | flops | bytes accessed | tf_op | source)
XLA Modules:
  0.0 484.3 jit_solution(978483173474145397)
XLA Ops:
  7.2 0.8 compare_select_fusion
  8.0 0.6 collective-permute-start.1
  8.7 4.4 collective-permute-start
  13.1 0.7 collective-permute-start.3
  13.8 1.3 collective-permute-start.2
  15.1 1.6 select_convert_fusion.1.qtag_ref
  16.7 7.3 %project.3 = (bf16[1024,768]{1,0:T(8,128)(2,1)}, bf16[1024,768]{1,0:T(8,128)(2,1)}, bf16[1024,768]{1,0:T(8,128)(2,1)}) custom-call(bf16[1024,768]{1,0:T(8,128)(2,1)} %own_in.5, bf16[768,768]{1,0:T(8,128)(2,1)} %w_key.11, bf16[768,768]{1,0:T(8,128)(2,1)} %w_value.11, f32[768]{0:T(1024)} %b_value.5, bf16[768,768]{1,0:T(8,128)(2,1)} %refs_1_.3, f32[768]{0:T(1024)} %refs_1_.2), custom_call_target="tpu_custom_call" | custom-call | flops 3623878656 | bytes 7864320 | tf_op jit(solution)/shard_map/project/pallas_call | solution.py:323
  24.3 1.0 copy.46.mask
  26.2 2.1 select_convert_fusion.ktag_ref
  28.3 1.1 copy-done.24
  29.4 5.6 %project.4 = (bf16[1024,768]{1,0:T(8,128)(2,1)}, bf16[1024,768]{1,0:T(8,128)(2,1)}) custom-call(bf16[1024,768]{1,0:T(8,128)(2,1)} %copy-done.24, bf16[768,768]{1,0:T(8,128)(2,1)} %w_key.11, bf16[768,768]{1,0:T(8,128)(2,1)} %w_value.11, f32[768]{0:T(1024)} %b_value.5), custom_call_target="tpu_custom_call" | custom-call | flops 3623878656 | bytes 7864320 | tf_op jit(solution)/shard_map/project/pallas_call | solution.py:323
  35.0 1.1 copy-done.23
  36.2 5.6 %project.5 = (bf16[1024,768]{1,0:T(8,128)(2,1)}, bf16[1024,768]{1,0:T(8,128)(2,1)}) custom-call(bf16[1024,768]{1,0:T(8,128)(2,1)} %copy-done.23, bf16[768,768]{1,0:T(8,128)(2,1)} %w_key.11, bf16[768,768]{1,0:T(8,128)(2,1)} %w_value.11, f32[768]{0:T(1024)} %b_value.5), custom_call_target="tpu_custom_call" | custom-call | flops 3623878656 | bytes 7864320 | tf_op jit(solution)/shard_map/project/pallas_call | solution.py:323
  41.7 63.1 %attend.1 = (bf16[1024,768]{1,0:T(8,128)(2,1)}, bf16[1024,768]{1,0:T(8,128)(2,1)}) custom-call(s32[3]{0:T(128)} %and_select_fusion.1.tiles, bf16[1024,768]{1,0:T(8,128)(2,1)} %get-tuple-element.94.q_ref, bf16[1024,768]{1,0:T(8,128)(2,1)} %get-tuple-element.95.k_own, bf16[1024,768]{1,0:T(8,128)(2,1)} %get-tuple-element.96.k_mate, ...), custom_call_target="tpu_custom_call" | custom-call | flops 40000000000 | bytes 16777216 | tf_op jit(solution)/shard_map/attend/pallas_call | solution.py:152
  104.8 39.0 %dense.1 = (bf16[1024,768]{1,0:T(8,128)(2,1)}, bf16[768,1024]{1,0:T(8,128)(2,1)}, bf16[768,1024]{1,0:T(8,128)(2,1)}, bf16[768,1024]{1,0:T(8,128)(2,1)}, bf16[102...) custom-call(bf16[1024,768]{1,0:T(8,128)(2,1)} %own_in.5, ...), custom_call_target="tpu_custom_call" | custom-call | flops 40000000000 | bytes 41943040 | tf_op jit(solution)/shard_map/dense/pallas_call | solution.py:414
  143.8 19.0 %products.1 = bf16[768,6912]{1,0:T(8,128)(2,1)} custom-call(bf16[768,1024]{1,0:T(8,128)(2,1)} %get-tuple-element.105.low, bf16[768,1024]{1,0:T(8,128)(2,1)} %get-tuple-element.106.mixed, bf16[768,1024]{1,0:T(8,128)(2,1)} %get-tuple-element.107.d_branch, bf16[1024,3072]{1,0:T(8,128)(2,1)} %get-tuple-element.108.d_upper, ...), custom_call_target="tpu_custom_call" | custom-call | flops 10871635968 | bytes 47185920 | tf_op jit(solution)/shard_map/products/pallas_call | solution.py:546
  163.0 1.0 copy-done.1
  164.0 1.4 copy-done.13
  165.4 27.0 %attend_back.3 = (f32[16,768]{1,0:T(8,128)S(1)}, bf16[1024,768]{1,0:T(8,128)(2,1)S(1)}, bf16[3072,768]{1,0:T(8,128)(2,1)}, bf16[3072,768]{1,0:T(8,128)(2,1)}, bf16[768,768]{1,0:T(8,128)(2,1)S(1)}) custom-call(s32[4]{0:T(128)S(1)} %add.169.qbits, s32[6]{0:T(128)S(1)} %add.170.kbits, ...), custom_call_target="tpu_custom_call", output_to_operand_aliasing={{0}: (16, {})} | custom-call | flops 35999997952 | bytes 8388608 | tf_op jit(solution)/shard_map/attend_back/pallas_call | solution.py:286
  192.5 32.1 %collective-permute-start.4 = (bf16[384,768]{1,0:T(8,128)(2,1)S(1)}, bf16[384,768]{1,0:T(8,128)(2,1)S(1)}, u32[]{:S(2)}, u32[]{:S(2)}) collective-permute-start(bf16[384,768]{1,0:T(8,128)(2,1)S(1)} %get-tuple-element.189.refs_4_), channel_id=1, source_target_pairs={{0,1},{1,0},{2,3},{3,2},{4,5},{5,4},{6,7},{7,6},{8,9},{9,8},{10,11... | collective-permute-start | bytes 1769480 | tf_op jit(solution)/shard_map/ppermute | solution.py:468
  224.6 27.0 %attend_back.4 = (f32[16,768]{1,0:T(8,128)S(1)}, bf16[1024,768]{1,0:T(8,128)(2,1)S(1)}, bf16[3072,768]{1,0:T(8,128)(2,1)}, bf16[3072,768]{1,0:T(8,128)(2,1)}, bf16[768,768]{1,0:T(8,128)(2,1)S(1)}) custom-call(s32[4]{0:T(128)S(1)} %add.169.qbits, s32[6]{0:T(128)S(1)} %add.170.kbits, ...), custom_call_target="tpu_custom_call", output_to_operand_aliasing={{0}: (16, {}), {1}: (17, {}), {2}: (18, {}), {3}: (19, {})} | custom-call | flops 35999997952 | bytes 8388608 | tf_op jit(solution)/shard_map/attend_back/pallas_call | solution.py:286
  251.7 1.0 constant_dynamic-slice_fusion.1
  252.6 11.5 %collective-permute-start.8 = (bf16[384,768]{1,0:T(8,128)(2,1)}, bf16[384,768]{1,0:T(8,128)(2,1)}, u32[]{:S(2)}, u32[]{:S(2)}) collective-permute-start(bf16[384,768]{1,0:T(8,128)(2,1)} %get-tuple-element.187.refs_8_), channel_id=1, source_target_pairs={{0,1},{1,0},{2,3},{3,2},{4,5},{5,4},{6,7},{7,6},{8,9},{9,8},{10,11... | collective-permute-start | bytes 1769480 | tf_op jit(solution)/shard_map/ppermute | solution.py:468
  264.4 0.8 constant_dynamic-slice_fusion.3
  265.2 0.8 copy-done.6
  266.0 26.9 %attend_back.5 = (f32[16,768]{1,0:T(8,128)S(1)}, bf16[1024,768]{1,0:T(8,128)(2,1)S(1)}, bf16[3072,768]{1,0:T(8,128)(2,1)}, bf16[3072,768]{1,0:T(8,128)(2,1)}, bf16[768,768]{1,0:T(8,128)(2,1)S(1)}) custom-call(s32[4]{0:T(128)S(1)} %copy-done.10, s32[6]{0:T(128)S(1)} %copy-done.12, ...), custom_call_target="tpu_custom_call", output_to_operand_aliasing={{0}: (16, {}), {1}: (17, {}), {2}: (18, {}), {3}: (19, {})} | custom-call | flops 35999997952 | bytes 8388608 | tf_op jit(solution)/shard_map/attend_back/pallas_call | solution.py:286
  293.0 11.7 %collective-permute-start.9 = (bf16[384,768]{1,0:T(8,128)(2,1)S(1)}, bf16[384,768]{1,0:T(8,128)(2,1)}, u32[]{:S(2)}, u32[]{:S(2)}) collective-permute-start(bf16[384,768]{1,0:T(8,128)(2,1)S(1)} %constant_dynamic-slice_fusion), channel_id=1, source_target_pairs={{0,1},{1,0},{2,3},{3,2},{4,5},{5,4},{6,7},{7,6},{8,9},{9,8},{10,11... | collective-permute-start | bytes 1769480 | tf_op jit(solution)/shard_map/ppermute | solution.py:468
  304.7 3.5 collective-permute-start.5
  308.2 5.9 %back_product.3 = bf16[1024,768]{1,0:T(8,128)(2,1)} custom-call(bf16[3072,768]{1,0:T(8,128)(2,1)} %get-tuple-element.146.dk, bf16[3072,768]{1,0:T(8,128)(2,1)} %get-tuple-element.138.dv, bf16[768,768]{1,0:T(8,128)(2,1)} %w_key.11, bf16[768,768]{1,0:T(8,128)(2,1)} %w_value.11), custom_call_target="tpu_custom_call" | custom-call | flops 2415919104 | bytes 7864320 | tf_op jit(solution)/shard_map/back_product/pallas_call | solution.py:448
  314.2 2.2 collective-permute-done.5
  316.4 1.2 add_convert_fusion.1
  317.7 1.2 add_convert_fusion
  319.1 1.0 fusion
  320.1 25.5 %reduce-scatter.2.cloned.1.call-done = bf16[24,6912]{1,0:T(8,128)(2,1)} async-done(((bf16[768,6912]{1,0:T(8,128)(2,1)}), bf16[24,6912]{1,0:T(8,128)(2,1)}) %reduce-scatter.2.cloned.1.call-update) | async-done | bytes 331792 | tf_op jit(solution)/shard_map/reduce_scatter | solution.py:655
  345.7 2.7 collective-permute-start.12
  348.4 0.8 collective-permute-start.13
  349.2 1.1 add_convert_fusion.4
  350.4 1.8 collective-permute-start.18
  352.2 6.1 %back_product.4 = bf16[1024,768]{1,0:T(8,128)(2,1)} custom-call(bf16[3072,768]{1,0:T(8,128)(2,1)} %get-tuple-element.146.dk, bf16[3072,768]{1,0:T(8,128)(2,1)} %get-tuple-element.138.dv, bf16[768,768]{1,0:T(8,128)(2,1)} %w_key.11, bf16[768,768]{1,0:T(8,128)(2,1)} %w_value.11), custom_call_target="tpu_custom_call" | custom-call | flops 2415919104 | bytes 7864320 | tf_op jit(solution)/shard_map/back_product/pallas_call | solution.py:448
  358.3 6.4 %collective-permute-done.13 = bf16[104,1536]{1,0:T(8,128)(2,1)} collective-permute-done((bf16[104,1536]{1,0:T(8,128)(2,1)}, bf16[104,1536]{1,0:T(8,128)(2,1)}, u32[]{:S(2)}, u32[]{:S(2)}) %collective-permute-start.13) | collective-permute-done | bytes 319520 | tf_op jit(solution)/shard_map/ppermute | solution.py:468
  364.7 0.8 add_convert_fusion.7
  366.0 1.1 add_convert_fusion.3
  367.3 1.9 collective-permute-start.16
  369.1 2.6 collective-permute-start.14
  371.7 9.5 %back_product.5 = bf16[1024,768]{1,0:T(8,128)(2,1)} custom-call(bf16[3072,768]{1,0:T(8,128)(2,1)} %get-tuple-element.146.dk, bf16[3072,768]{1,0:T(8,128)(2,1)} %get-tuple-element.138.dv, bf16[768,768]{1,0:T(8,128)(2,1)} %w_key.11, bf16[768,768]{1,0:T(8,128)(2,1)} %w_value.11, bf16[1024,768]{1,0:T(8,128)(2,1)} %copy-done, bf16[768,768]{1,0:T(8,128)(2,1)} %refs_1_.3, ...), custom_call_target="tpu_custom_call" | custom-call | flops 3623878656 | bytes 7864320 | tf_op jit(solution)/shard_map/back_product/pallas_call | solution.py:448
  381.3 3.8 collective-permute-done.14
  385.2 2.1 collective-permute-start.20
  387.3 2.3 collective-permute-start.19
  389.5 8.2 %collective-permute-done.21 = bf16[24,2304]{1,0:T(8,128)(2,1)S(1)} collective-permute-done((bf16[24,2304]{1,0:T(8,128)(2,1)S(1)}, bf16[24,2304]{1,0:T(8,128)(2,1)S(1)}, u32[]{:S(2)}, u32[]{:S(2)}) %collective-permute-start.21) | collective-permute-done | bytes 110624 | tf_op jit(solution)/shard_map/ppermute | solution.py:468
  397.7 2.9 collective-permute-done.19
  400.8 1.6 collective-permute-start.24
  402.4 8.1 %collective-permute-start.23 = (bf16[96,2304]{1,0:T(8,128)(2,1)S(1)}, bf16[96,2304]{1,0:T(8,128)(2,1)S(1)}, u32[]{:S(2)}, u32[]{:S(2)}) collective-permute-start(bf16[96,2304]{1,0:T(8,128)(2,1)S(1)} %pad_maximum_fusion.2), channel_id=1, source_target_pairs={{0,2},{1,3},{2,0},{3,1},{4,6},{5,7},{6,4},{7,5},{8,10},{9,11},{10,... | collective-permute-start | bytes 1327112 | tf_op jit(solution)/shard_map/ppermute | solution.py:468
  410.5 25.6 %collective-permute-done.23 = bf16[96,2304]{1,0:T(8,128)(2,1)S(1)} collective-permute-done((bf16[96,2304]{1,0:T(8,128)(2,1)S(1)}, bf16[96,2304]{1,0:T(8,128)(2,1)S(1)}, u32[]{:S(2)}, u32[]{:S(2)}) %collective-permute-start.23) | collective-permute-done | bytes 442400 | tf_op jit(solution)/shard_map/ppermute | solution.py:468
  436.1 4.1 collective-permute-done.22
  440.8 1.3 pad_maximum_fusion.1
  442.1 0.8 add_convert_fusion.6
  443.0 0.6 copy-done.22
  443.6 0.6 slice.104
  444.2 1.3 reshape.90
  445.5 1.5 convert_reduce_fusion
  447.0 0.7 broadcast_select_fusion.1
  447.9 3.0 split.1
  450.9 13.8 %all-gather.2.cloned.1.call-done.from_down.from_up.from_out = bf16[768,6912]{1,0:T(8,128)(2,1)} async-done(((bf16[24,6912]{1,0:T(8,128)(2,1)}), bf16[768,6912]{1,0:T(8,128)(2,1)}) %all-gather.2.cloned.1.call-update) | async-done | bytes 10616848 | tf_op jit(solution)/shard_map/all_gather | solution.py:693
  464.7 12.3 %place.1 = (f32[3072,768]{1,0:T(8,128)}, f32[768,3072]{1,0:T(8,128)}, f32[768,768]{1,0:T(8,128)}) custom-call(bf16[768,6912]{1,0:T(8,128)(2,1)} %all-gather.2.cloned.1.call-done.from_down.from_up.from_out, bf16[768,6912]{1,0:T(8,128)(2,1)} %all-gather.2.cloned.1.call-done.from_down.from_up.from_out, ...), custom_call_target="tpu_custom_call" | custom-call | bytes 28311552 | tf_op jit(solution)/shard_map/place/pallas_call | solution.py:570
  (112 shorter events, 3.7 us)
Async XLA Ops:
  7.2 338.4 %reduce-scatter.2.cloned.1.call-start = ((), (), s32[]{:S(2)}) async-start(), calls=%async_computation.1 | async-start | bytes 10948608 | tf_op jit(solution)/shard_map/reduce_scatter | solution.py:655
  8.0 17.3 %collective-permute-start.1 = (s32[1024]{0:T(1024)S(1)}, s32[1024]{0:T(1024)S(1)}, u32[]{:S(2)}, u32[]{:S(2)}) collective-permute-start(s32[1024]{0:T(1024)S(1)} %get-tuple-element.178), channel_id=1, source_target_pairs={{1,2},{2,1},{5,6},{6,5},{9,10},{10,9},{13,14},{14,13},{17,18},{18,... | collective-permute-start | bytes 12296 | tf_op jit(solution)/shard_map/ppermute | solution.py:630
  8.7 16.6 %collective-permute-start = (s32[1024]{0:T(1024)S(1)}, s32[1024]{0:T(1024)S(1)}, u32[]{:S(2)}, u32[]{:S(2)}) collective-permute-start(s32[1024]{0:T(1024)S(1)} %get-tuple-element.178), channel_id=1, source_target_pairs={{0,1},{1,0},{2,3},{3,2},{4,5},{5,4},{6,7},{7,6},{8,9},{9,8},{10,11... | collective-permute-start | bytes 12296 | tf_op jit(solution)/shard_map/ppermute | solution.py:629
  13.1 22.0 %collective-permute-start.3 = (bf16[1024,768]{1,0:T(8,128)(2,1)}, bf16[1024,768]{1,0:T(8,128)(2,1)S(1)}, u32[]{:S(2)}, u32[]{:S(2)}) collective-permute-start(bf16[1024,768]{1,0:T(8,128)(2,1)} %own_in.5), channel_id=1, source_target_pairs={{1,2},{2,1},{5,6},{6,5},{9,10},{10,9},{13,14},{14,13},{17,18},{18,... | collective-permute-start | bytes 4718600 | tf_op jit(solution)/shard_map/ppermute | solution.py:630
  13.8 14.5 %collective-permute-start.2 = (bf16[1024,768]{1,0:T(8,128)(2,1)}, bf16[1024,768]{1,0:T(8,128)(2,1)S(1)}, u32[]{:S(2)}, u32[]{:S(2)}) collective-permute-start(bf16[1024,768]{1,0:T(8,128)(2,1)} %own_in.5), channel_id=1, source_target_pairs={{0,1},{1,0},{2,3},{3,2},{4,5},{5,4},{6,7},{7,6},{8,9},{9,8},{10,11... | collective-permute-start | bytes 4718600 | tf_op jit(solution)/shard_map/ppermute | solution.py:629
  25.3 199.4 %copy-start.9 = (s32[4]{0:T(128)}, s32[4]{0:T(128)S(1)}, u32[]{:S(2)}) copy-start(s32[4]{0:T(128)S(1)} %add.169.qbits) | copy-start | bytes 52
  25.5 199.1 %copy-start.11 = (s32[6]{0:T(128)}, s32[6]{0:T(128)S(1)}, u32[]{:S(2)}) copy-start(s32[6]{0:T(128)S(1)} %add.170.kbits) | copy-start | bytes 76
  28.3 1.1 copy-start.24
  35.0 1.1 copy-start.23
  162.9 1.1 copy-start.1
  162.9 1.1 copy-start.4
  162.9 301.8 %all-gather.2.cloned.1.call-start = ((), (), s32[]{:S(2)}) async-start(), calls=%async_computation.2 | async-start | bytes 10948608 | tf_op jit(solution)/shard_map/all_gather | solution.py:693
  164.0 1.4 copy-start.13
  192.5 71.7 %collective-permute-start.4 = (bf16[384,768]{1,0:T(8,128)(2,1)S(1)}, bf16[384,768]{1,0:T(8,128)(2,1)S(1)}, u32[]{:S(2)}, u32[]{:S(2)}) collective-permute-start(bf16[384,768]{1,0:T(8,128)(2,1)S(1)} %get-tuple-element.189.refs_4_), channel_id=1, source_target_pairs={{0,1},{1,0},{2,3},{3,2},{4,5},{5,4},{6,7},{7,6},{8,9},{9,8},{10,11... | collective-permute-start | bytes 1769480 | tf_op jit(solution)/shard_map/ppermute | solution.py:468
  251.7 13.5 %copy-start.5 = (f32[16,768]{1,0:T(8,128)}, f32[16,768]{1,0:T(8,128)S(1)}, u32[]{:S(2)}) copy-start(f32[16,768]{1,0:T(8,128)S(1)} %get-tuple-element.122.sums_in) | copy-start | bytes 147460
  252.6 12.5 %copy-start.10 = (s32[4]{0:T(128)S(1)}, s32[4]{0:T(128)}, u32[]{:S(2)}) copy-start(s32[4]{0:T(128)} %copy-done.9) | copy-start | bytes 52
  252.6 12.5 %copy-start.12 = (s32[6]{0:T(128)S(1)}, s32[6]{0:T(128)}, u32[]{:S(2)}) copy-start(s32[6]{0:T(128)} %copy-done.11) | copy-start | bytes 76
  252.6 63.8 %collective-permute-start.8 = (bf16[384,768]{1,0:T(8,128)(2,1)}, bf16[384,768]{1,0:T(8,128)(2,1)}, u32[]{:S(2)}, u32[]{:S(2)}) collective-permute-start(bf16[384,768]{1,0:T(8,128)(2,1)} %get-tuple-element.187.refs_8_), channel_id=1, source_target_pairs={{0,1},{1,0},{2,3},{3,2},{4,5},{5,4},{6,7},{7,6},{8,9},{9,8},{10,11... | collective-permute-start | bytes 1769480 | tf_op jit(solution)/shard_map/ppermute | solution.py:468
  265.2 27.8 %copy-start.2 = (bf16[96,768]{1,0:T(8,128)(2,1)}, bf16[96,768]{1,0:T(8,128)(2,1)S(1)}, u32[]{:S(2)}) copy-start(bf16[96,768]{1,0:T(8,128)(2,1)S(1)} %get-tuple-element.194.refs_3_) | copy-start | bytes 442372
  265.2 0.8 copy-start.6
  292.9 15.2 %copy-start.7 = (f32[16,768]{1,0:T(8,128)}, f32[16,768]{1,0:T(8,128)S(1)}, u32[]{:S(2)}) copy-start(f32[16,768]{1,0:T(8,128)S(1)} %get-tuple-element.136) | copy-start | bytes 147460
  293.0 21.1 %copy-start = (bf16[1024,768]{1,0:T(8,128)(2,1)}, bf16[1024,768]{1,0:T(8,128)(2,1)S(1)}, u32[]{:S(2)}) copy-start(bf16[1024,768]{1,0:T(8,128)(2,1)S(1)} %get-tuple-element.150.refs_0_) | copy-start | bytes 4718596
  293.0 24.7 %collective-permute-start.9 = (bf16[384,768]{1,0:T(8,128)(2,1)S(1)}, bf16[384,768]{1,0:T(8,128)(2,1)}, u32[]{:S(2)}, u32[]{:S(2)}) collective-permute-start(bf16[384,768]{1,0:T(8,128)(2,1)S(1)} %constant_dynamic-slice_fusion), channel_id=1, source_target_pairs={{0,1},{1,0},{2,3},{3,2},{4,5},{5,4},{6,7},{7,6},{8,9},{9,8},{10,11... | collective-permute-start | bytes 1769480 | tf_op jit(solution)/shard_map/ppermute | solution.py:468
  304.7 9.4 %collective-permute-start.7 = (bf16[96,768]{1,0:T(8,128)(2,1)}, bf16[96,768]{1,0:T(8,128)(2,1)S(1)}, u32[]{:S(2)}, u32[]{:S(2)}) collective-permute-start(bf16[96,768]{1,0:T(8,128)(2,1)} %get-tuple-element.191.refs_6_), channel_id=1, source_target_pairs={{0,6},{1,7},{2,4},{3,5},{4,2},{5,3},{6,0},{7,1},{8,14},{9,15},{10,... | collective-permute-start | bytes 442376 | tf_op jit(solution)/shard_map/ppermute | solution.py:468
  304.7 9.5 %collective-permute-start.6 = (bf16[96,768]{1,0:T(8,128)(2,1)}, bf16[96,768]{1,0:T(8,128)(2,1)}, u32[]{:S(2)}, u32[]{:S(2)}) collective-permute-start(bf16[96,768]{1,0:T(8,128)(2,1)} %get-tuple-element.192.refs_5_), channel_id=1, source_target_pairs={{0,4},{1,5},{2,6},{3,7},{4,0},{5,1},{6,2},{7,3},{8,12},{9,13},{10,... | collective-permute-start | bytes 442376 | tf_op jit(solution)/shard_map/ppermute | solution.py:468
  304.7 11.7 %collective-permute-start.5 = (bf16[96,768]{1,0:T(8,128)(2,1)}, bf16[96,768]{1,0:T(8,128)(2,1)}, u32[]{:S(2)}, u32[]{:S(2)}) collective-permute-start(bf16[96,768]{1,0:T(8,128)(2,1)} %get-tuple-element.193.refs_4_), channel_id=1, source_target_pairs={{0,2},{1,3},{2,0},{3,1},{4,6},{5,7},{6,4},{7,5},{8,10},{9,11},{10,... | collective-permute-start | bytes 442376 | tf_op jit(solution)/shard_map/ppermute | solution.py:468
  314.1 3.6 copy-start.8
  314.1 4.9 %copy-start.19 = (bf16[96,768]{1,0:T(8,128)(2,1)}, bf16[96,768]{1,0:T(8,128)(2,1)S(1)}, u32[]{:S(2)}) copy-start(bf16[96,768]{1,0:T(8,128)(2,1)S(1)} %collective-permute-done.7) | copy-start | bytes 442372
  314.1 3.6 collective-permute-start.10
  317.7 1.4 copy-start.20
  319.1 30.1 %copy-start.3 = (bf16[96,768]{1,0:T(8,128)(2,1)S(1)}, bf16[96,768]{1,0:T(8,128)(2,1)}, u32[]{:S(2)}) copy-start(bf16[96,768]{1,0:T(8,128)(2,1)} %copy-done.2) | copy-start | bytes 442372
  319.1 31.3 %copy-start.14 = (bf16[1024,768]{1,0:T(8,128)(2,1)S(1)}, bf16[1024,768]{1,0:T(8,128)(2,1)}, u32[]{:S(2)}) copy-start(bf16[1024,768]{1,0:T(8,128)(2,1)} %back_product.3) | copy-start | bytes 4718596
  345.7 12.6 %collective-permute-start.11 = (bf16[104,1536]{1,0:T(8,128)(2,1)}, bf16[104,1536]{1,0:T(8,128)(2,1)S(1)}, u32[]{:S(2)}, u32[]{:S(2)}) collective-permute-start(bf16[104,1536]{1,0:T(8,128)(2,1)} %get-tuple-element.141), channel_id=1, source_target_pairs={{0,2},{1,3},{2,0},{3,1},{4,6},{5,7},{6,4},{7,5},{8,10},{9,11},{10,... | collective-permute-start | bytes 958472 | tf_op jit(solution)/shard_map/ppermute | solution.py:468
  345.7 12.5 %collective-permute-start.12 = (bf16[104,1536]{1,0:T(8,128)(2,1)}, bf16[104,1536]{1,0:T(8,128)(2,1)S(1)}, u32[]{:S(2)}, u32[]{:S(2)}) collective-permute-start(bf16[104,1536]{1,0:T(8,128)(2,1)} %get-tuple-element.142), channel_id=1, source_target_pairs={{0,4},{1,5},{2,6},{3,7},{4,0},{5,1},{6,2},{7,3},{8,12},{9,13},{10,... | collective-permute-start | bytes 958472 | tf_op jit(solution)/shard_map/ppermute | solution.py:468
  348.4 16.3 %collective-permute-start.13 = (bf16[104,1536]{1,0:T(8,128)(2,1)}, bf16[104,1536]{1,0:T(8,128)(2,1)}, u32[]{:S(2)}, u32[]{:S(2)}) collective-permute-start(bf16[104,1536]{1,0:T(8,128)(2,1)} %get-tuple-element.143), channel_id=1, source_target_pairs={{0,6},{1,7},{2,4},{3,5},{4,2},{5,3},{6,0},{7,1},{8,14},{9,15},{10,... | collective-permute-start | bytes 958472 | tf_op jit(solution)/shard_map/ppermute | solution.py:468
  350.4 14.3 %copy-start.21 = (bf16[8,768]{1,0:T(8,128)(2,1)S(1)}, bf16[8,768]{1,0:T(8,128)(2,1)}, u32[]{:S(2)}) copy-start(bf16[8,768]{1,0:T(8,128)(2,1)} %copy-done.20) | copy-start | bytes 36868
  350.4 21.3 %collective-permute-start.18 = (bf16[1024,768]{1,0:T(8,128)(2,1)S(1)}, bf16[1024,768]{1,0:T(8,128)(2,1)}, u32[]{:S(2)}, u32[]{:S(2)}) collective-permute-start(bf16[1024,768]{1,0:T(8,128)(2,1)S(1)} %copy-done.14), channel_id=1, source_target_pairs={{1,2},{2,1},{5,6},{6,5},{9,10},{10,9},{13,14},{14,13},{17,18},{18,... | collective-permute-start | bytes 4718600 | tf_op jit(solution)/shard_map/ppermute | solution.py:630
  364.7 7.0 %collective-permute-start.17 = (bf16[1024,768]{1,0:T(8,128)(2,1)}, bf16[1024,768]{1,0:T(8,128)(2,1)}, u32[]{:S(2)}, u32[]{:S(2)}) collective-permute-start(bf16[1024,768]{1,0:T(8,128)(2,1)} %back_product.4), channel_id=1, source_target_pairs={{0,1},{1,0},{2,3},{3,2},{4,5},{5,4},{6,7},{7,6},{8,9},{9,8},{10,11... | collective-permute-start | bytes 4718600 | tf_op jit(solution)/shard_map/ppermute | solution.py:629
  365.4 0.6 copy-start.15
  367.3 14.0 %collective-permute-start.16 = (bf16[32,2304]{1,0:T(8,128)(2,1)S(1)}, bf16[32,2304]{1,0:T(8,128)(2,1)S(1)}, u32[]{:S(2)}, u32[]{:S(2)}) collective-permute-start(bf16[32,2304]{1,0:T(8,128)(2,1)S(1)} %get-tuple-element.204), channel_id=1, source_target_pairs={{0,24},{1,25},{2,26},{3,27},{4,28},{5,29},{6,30},{7,31},{8,16},{9,... | collective-permute-start | bytes 442376 | tf_op jit(solution)/shard_map/ppermute | solution.py:468
  369.1 12.1 %collective-permute-start.15 = (bf16[32,2304]{1,0:T(8,128)(2,1)S(1)}, bf16[32,2304]{1,0:T(8,128)(2,1)S(1)}, u32[]{:S(2)}, u32[]{:S(2)}) collective-permute-start(bf16[32,2304]{1,0:T(8,128)(2,1)S(1)} %get-tuple-element.205), channel_id=1, source_target_pairs={{0,8},{1,9},{2,10},{3,11},{4,12},{5,13},{6,14},{7,15},{8,0},{9,1},... | collective-permute-start | bytes 442376 | tf_op jit(solution)/shard_map/ppermute | solution.py:468
  369.1 15.9 %collective-permute-start.14 = (bf16[32,2304]{1,0:T(8,128)(2,1)S(1)}, bf16[32,2304]{1,0:T(8,128)(2,1)S(1)}, u32[]{:S(2)}, u32[]{:S(2)}) collective-permute-start(bf16[32,2304]{1,0:T(8,128)(2,1)S(1)} %get-tuple-element.206), channel_id=1, source_target_pairs={{0,16},{1,17},{2,18},{3,19},{4,20},{5,21},{6,22},{7,23},{8,24},{9,... | collective-permute-start | bytes 442376 | tf_op jit(solution)/shard_map/ppermute | solution.py:468
  381.2 58.9 %copy-start.16 = (bf16[32,2304]{1,0:T(8,128)(2,1)}, bf16[32,2304]{1,0:T(8,128)(2,1)S(1)}, u32[]{:S(2)}) copy-start(bf16[32,2304]{1,0:T(8,128)(2,1)S(1)} %collective-permute-done.16) | copy-start | bytes 442372
  381.3 58.9 %copy-start.17 = (bf16[32,2304]{1,0:T(8,128)(2,1)}, bf16[32,2304]{1,0:T(8,128)(2,1)S(1)}, u32[]{:S(2)}) copy-start(bf16[32,2304]{1,0:T(8,128)(2,1)S(1)} %collective-permute-done.15) | copy-start | bytes 442372
  385.0 55.1 %copy-start.18 = (bf16[32,2304]{1,0:T(8,128)(2,1)}, bf16[32,2304]{1,0:T(8,128)(2,1)S(1)}, u32[]{:S(2)}) copy-start(bf16[32,2304]{1,0:T(8,128)(2,1)S(1)} %collective-permute-done.14) | copy-start | bytes 442372
  385.1 12.6 %collective-permute-start.21 = (bf16[24,2304]{1,0:T(8,128)(2,1)S(1)}, bf16[24,2304]{1,0:T(8,128)(2,1)S(1)}, u32[]{:S(2)}, u32[]{:S(2)}) collective-permute-start(bf16[24,2304]{1,0:T(8,128)(2,1)S(1)} %add_convert_fusion.5), channel_id=1, source_target_pairs={{0,8},{1,9},{2,10},{3,11},{4,12},{5,13},{6,14},{7,15},{8,0},{9,1},... | collective-permute-start | bytes 331784 | tf_op jit(solution)/shard_map/ppermute | solution.py:468
  385.2 12.6 %collective-permute-start.20 = (bf16[24,2304]{1,0:T(8,128)(2,1)S(1)}, bf16[24,2304]{1,0:T(8,128)(2,1)S(1)}, u32[]{:S(2)}, u32[]{:S(2)}) collective-permute-start(bf16[24,2304]{1,0:T(8,128)(2,1)S(1)} %add_convert_fusion.5), channel_id=1, source_target_pairs={{0,16},{1,17},{2,18},{3,19},{4,20},{5,21},{6,22},{7,23},{8,24},{9,... | collective-permute-start | bytes 331784 | tf_op jit(solution)/shard_map/ppermute | solution.py:468
  387.3 13.4 %collective-permute-start.19 = (bf16[24,2304]{1,0:T(8,128)(2,1)S(1)}, bf16[24,2304]{1,0:T(8,128)(2,1)S(1)}, u32[]{:S(2)}, u32[]{:S(2)}) collective-permute-start(bf16[24,2304]{1,0:T(8,128)(2,1)S(1)} %add_convert_fusion.5), channel_id=1, source_target_pairs={{0,24},{1,25},{2,26},{3,27},{4,28},{5,29},{6,30},{7,31},{8,16},{9,... | collective-permute-start | bytes 331784 | tf_op jit(solution)/shard_map/ppermute | solution.py:468
  400.8 9.7 %collective-permute-start.24 = (bf16[96,2304]{1,0:T(8,128)(2,1)S(1)}, bf16[96,2304]{1,0:T(8,128)(2,1)S(1)}, u32[]{:S(2)}, u32[]{:S(2)}) collective-permute-start(bf16[96,2304]{1,0:T(8,128)(2,1)S(1)} %pad_maximum_fusion.2), channel_id=1, source_target_pairs={{0,4},{1,5},{2,6},{3,7},{4,0},{5,1},{6,2},{7,3},{8,12},{9,13},{10,... | collective-permute-start | bytes 1327112 | tf_op jit(solution)/shard_map/ppermute | solution.py:468
  402.4 33.7 %collective-permute-start.23 = (bf16[96,2304]{1,0:T(8,128)(2,1)S(1)}, bf16[96,2304]{1,0:T(8,128)(2,1)S(1)}, u32[]{:S(2)}, u32[]{:S(2)}) collective-permute-start(bf16[96,2304]{1,0:T(8,128)(2,1)S(1)} %pad_maximum_fusion.2), channel_id=1, source_target_pairs={{0,2},{1,3},{2,0},{3,1},{4,6},{5,7},{6,4},{7,5},{8,10},{9,11},{10,... | collective-permute-start | bytes 1327112 | tf_op jit(solution)/shard_map/ppermute | solution.py:468
  410.5 29.7 %collective-permute-start.22 = (bf16[96,2304]{1,0:T(8,128)(2,1)S(1)}, bf16[96,2304]{1,0:T(8,128)(2,1)S(1)}, u32[]{:S(2)}, u32[]{:S(2)}) collective-permute-start(bf16[96,2304]{1,0:T(8,128)(2,1)S(1)} %pad_maximum_fusion.2), channel_id=1, source_target_pairs={{0,6},{1,7},{2,4},{3,5},{4,2},{5,3},{6,0},{7,1},{8,14},{9,15},{10,... | collective-permute-start | bytes 1327112 | tf_op jit(solution)/shard_map/ppermute | solution.py:468
  442.1 4.8 %collective-permute-start.25 = (bf16[384,2304]{1,0:T(8,128)(2,1)}, bf16[384,2304]{1,0:T(8,128)(2,1)S(1)}, u32[]{:S(2)}, u32[]{:S(2)}) collective-permute-start(bf16[384,2304]{1,0:T(8,128)(2,1)} %pad_maximum_fusion.1), channel_id=1, source_target_pairs={{0,1},{1,0},{2,3},{3,2},{4,5},{5,4},{6,7},{7,6},{8,9},{9,8},{10,11... | collective-permute-start | bytes 5308424 | tf_op jit(solution)/shard_map/ppermute | solution.py:468
  443.0 0.6 copy-start.22
Sparse Core Ops, SparseCore 0:
  163.0 182.5 reduce-scatter.1
  348.5 116.1 all-gather.1
where the time goes:
time: 492 us; the launch traced here: 484 us
  Pallas kernels  257 us (52%)
  waiting for transfers between devices  92.5 us (19%)
  starting transfers between devices  90 us (18%)
  other arithmetic  17.6 us (4%)
  between operations  15.1 us (3%)
  local copies, waits for them, and re-layouts  11.7 us (2%)
    ppermute x20, starting transfers between devices, swapped(): return lax.ppermute(block, ALL, [(i, i ^ mask) for i in range(everyone())])  81 us
    pallas_call x3, Pallas kernels, attend_back(): pl.pallas_call(functools.partial(attend_back_kernel, tk), grid_spec=pltpu...  80.9 us
    pallas_call x1, Pallas kernels, attend(): pl.pallas_call(attend_kernel, grid_spec=pltpu.PrefetchScalarGridSpec(num_...  63.1 us
    ppermute x20, waiting for transfers between devices, swapped(): return lax.ppermute(block, ALL, [(i, i ^ mask) for i in range(everyone())])  53.2 us
    pallas_call x1, Pallas kernels, dense(): pl.pallas_call(functools.partial(dense_kernel, tf), grid=(rows // tr,), i...  39 us
    reduce_scatter x1, waiting for transfers between devices, body(): shares = lax.psum_scatter(products, ALL, scatter_dimension=0, tiled=True)  25.5 us
    pallas_call x3, Pallas kernels, back_product(): pl.pallas_call(back_kernel, grid=(rows // tr,), in_specs=[row(at), row(at...  21.5 us
    pallas_call x1, Pallas kernels, feed_forward_products(): pl.pallas_call(products_kernel, grid=(2 * count + 1,), in_specs=[once(d,...  19 us
  transfers between devices with their start and end apart: 28, of which 9 were waited for; matrix products, arithmetic and copies ran while one was open for 4% of the time, Pallas kernels for 24%

commit v1 on v0

--- a/solution.py
+++ b/solution.py
@@ -528,6 +528,17 @@
     return jnp.concatenate(parts)
 
 
+def both_ways(block, x, y):
+    rows, half = block.shape[0], block.shape[1] // 2
+    a, b = block[:, :half], block[:, half:]
+    a_theirs, b_theirs = swapped(a, y), swapped(b, x)
+    a, b = in_order([a, a_theirs], [y]), in_order([b, b_theirs], [x])
+    a_theirs, b_theirs = swapped(a, x), swapped(b, y)
+    a, b = in_order([a, a_theirs], [x]), in_order([b, b_theirs], [y])
+    b = b.reshape(2, 2, rows, half).transpose(1, 0, 2, 3).reshape(4 * rows, half)
+    return jnp.concatenate([a, b], axis=1)
+
+
 def products_kernel(low, mixed, d_branch, d_upper, d_att, active, made):
     step = pl.program_id(0)
     count = (pl.num_programs(0) - 1) // 2
@@ -706,6 +717,9 @@
     vectors = jnp.concatenate([vectors[:, :d], vectors[:, d:2 * d]]).astype(F32)
 
     for bits in reversed(direct):
+        if bits == [x, y]:
+            block = both_ways(block, x, y)
+            continue
         theirs = sent([block] * (len(masks_of(bits)) - 1), bits)
         block = in_order([block] + theirs, bits)
     grad_query, grad_key, grad_value = split_projections(block)

time: 492 us -> 487 us (0.990)
  waiting for transfers between devices: 92.5 us -> 63.8 us
  starting transfers between devices: 90 us -> 113 us
    reduce_scatter x1, waiting for transfers between devices: 25.5 us -> 2.26 us  [body(): shares = lax.psum_scatter(products, ALL, scatter_dimension=0, tiled=True)]
    ppermute x20 -> x21, starting transfers between devices: 81 us -> 104 us  [swapped(): return lax.ppermute(block, ALL, [(i, i ^ mask) for i in range(everyone())])]
    ppermute x20 -> x21, waiting for transfers between devices: 53.2 us -> 50.6 us  [swapped(): return lax.ppermute(block, ALL, [(i, i ^ mask) for i in range(everyone())])]
  transfers between devices with their start and end apart: 28 -> 29, of which waited for: 9 -> 13; matrix products, arithmetic and copies ran while one was open for 4% -> 5% of each run, Pallas kernels for 24% -> 25%
where the time goes in v1:
time: 487 us; the launch traced here: 479 us
  Pallas kernels  257 us (53%)
  starting transfers between devices  113 us (23%)
  waiting for transfers between devices  63.8 us (13%)
  other arithmetic  17.4 us (4%)
  between operations  15.1 us (3%)
  local copies, waits for them, and re-layouts  11.8 us (2%)
    ppermute x21, starting transfers between devices, swapped(): return lax.ppermute(block, ALL, [(i, i ^ mask) for i in range(everyone())])  104 us
    pallas_call x3, Pallas kernels, attend_back(): pl.pallas_call(functools.partial(attend_back_kernel, tk), grid_spec=pltpu...  80.9 us
    pallas_call x1, Pallas kernels, attend(): pl.pallas_call(attend_kernel, grid_spec=pltpu.PrefetchScalarGridSpec(num_...  63 us
    ppermute x21, waiting for transfers between devices, swapped(): return lax.ppermute(block, ALL, [(i, i ^ mask) for i in range(everyone())])  50.6 us
    pallas_call x1, Pallas kernels, dense(): pl.pallas_call(functools.partial(dense_kernel, tf), grid=(rows // tr,), i...  39 us
    pallas_call x3, Pallas kernels, back_product(): pl.pallas_call(back_kernel, grid=(rows // tr,), in_specs=[row(at), row(at...  21.6 us
    pallas_call x1, Pallas kernels, feed_forward_products(): pl.pallas_call(products_kernel, grid=(2 * count + 1,), in_specs=[once(d,...  19 us
    pallas_call x3, Pallas kernels, project(): pl.pallas_call(project_kernel, grid=(rows // tr,), in_specs=[tile, whole,...  18.4 us
  transfers between devices with their start and end apart: 29, of which 13 were waited for; matrix products, arithmetic and copies ran while one was open for 5% of the time, Pallas kernels for 25%

profile of v1, /device:TPU:0, one launch (start us, length us, event | category | flops | bytes accessed | tf_op | source)
XLA Modules:
  0.0 478.6 jit_solution(17000938830084715971)
XLA Ops:
  7.2 0.8 compare_select_fusion
  8.0 0.6 collective-permute-start.1
  8.7 4.4 collective-permute-start
  13.1 0.7 collective-permute-start.3
  13.8 1.3 collective-permute-start.2
  15.1 1.6 select_convert_fusion.1.qtag_ref
  16.7 7.3 %project.3 = (bf16[1024,768]{1,0:T(8,128)(2,1)}, bf16[1024,768]{1,0:T(8,128)(2,1)}, bf16[1024,768]{1,0:T(8,128)(2,1)}) custom-call(bf16[1024,768]{1,0:T(8,128)(2,1)} %own_in.5, bf16[768,768]{1,0:T(8,128)(2,1)} %w_key.11, bf16[768,768]{1,0:T(8,128)(2,1)} %w_value.11, f32[768]{0:T(1024)} %b_value.5, bf16[768,768]{1,0:T(8,128)(2,1)} %refs_1_.3, f32[768]{0:T(1024)} %refs_1_.2), custom_call_target="tpu_custom_call" | custom-call | flops 3623878656 | bytes 7864320 | tf_op jit(solution)/shard_map/project/pallas_call | solution.py:323
  24.3 1.0 copy.48.mask
  26.2 2.1 select_convert_fusion.ktag_ref
  28.3 1.1 copy-done.24
  29.5 5.6 %project.4 = (bf16[1024,768]{1,0:T(8,128)(2,1)}, bf16[1024,768]{1,0:T(8,128)(2,1)}) custom-call(bf16[1024,768]{1,0:T(8,128)(2,1)} %copy-done.24, bf16[768,768]{1,0:T(8,128)(2,1)} %w_key.11, bf16[768,768]{1,0:T(8,128)(2,1)} %w_value.11, f32[768]{0:T(1024)} %b_value.5), custom_call_target="tpu_custom_call" | custom-call | flops 3623878656 | bytes 7864320 | tf_op jit(solution)/shard_map/project/pallas_call | solution.py:323
  35.0 1.1 copy-done.23
  36.2 5.6 %project.5 = (bf16[1024,768]{1,0:T(8,128)(2,1)}, bf16[1024,768]{1,0:T(8,128)(2,1)}) custom-call(bf16[1024,768]{1,0:T(8,128)(2,1)} %copy-done.23, bf16[768,768]{1,0:T(8,128)(2,1)} %w_key.11, bf16[768,768]{1,0:T(8,128)(2,1)} %w_value.11, f32[768]{0:T(1024)} %b_value.5), custom_call_target="tpu_custom_call" | custom-call | flops 3623878656 | bytes 7864320 | tf_op jit(solution)/shard_map/project/pallas_call | solution.py:323
  41.7 63.0 %attend.1 = (bf16[1024,768]{1,0:T(8,128)(2,1)}, bf16[1024,768]{1,0:T(8,128)(2,1)}) custom-call(s32[3]{0:T(128)} %and_select_fusion.1.tiles, bf16[1024,768]{1,0:T(8,128)(2,1)} %get-tuple-element.94.q_ref, bf16[1024,768]{1,0:T(8,128)(2,1)} %get-tuple-element.95.k_own, bf16[1024,768]{1,0:T(8,128)(2,1)} %get-tuple-element.96.k_mate, ...), custom_call_target="tpu_custom_call" | custom-call | flops 40000000000 | bytes 16777216 | tf_op jit(solution)/shard_map/attend/pallas_call | solution.py:152
  104.8 39.0 %dense.1 = (bf16[1024,768]{1,0:T(8,128)(2,1)}, bf16[768,1024]{1,0:T(8,128)(2,1)}, bf16[768,1024]{1,0:T(8,128)(2,1)}, bf16[768,1024]{1,0:T(8,128)(2,1)}, bf16[102...) custom-call(bf16[1024,768]{1,0:T(8,128)(2,1)} %own_in.5, ...), custom_call_target="tpu_custom_call" | custom-call | flops 40000000000 | bytes 41943040 | tf_op jit(solution)/shard_map/dense/pallas_call | solution.py:414
  143.8 19.0 %products.1 = bf16[768,6912]{1,0:T(8,128)(2,1)} custom-call(bf16[768,1024]{1,0:T(8,128)(2,1)} %get-tuple-element.105.low, bf16[768,1024]{1,0:T(8,128)(2,1)} %get-tuple-element.106.mixed, bf16[768,1024]{1,0:T(8,128)(2,1)} %get-tuple-element.107.d_branch, bf16[1024,3072]{1,0:T(8,128)(2,1)} %get-tuple-element.108.d_upper, ...), custom_call_target="tpu_custom_call" | custom-call | flops 10871635968 | bytes 47185920 | tf_op jit(solution)/shard_map/products/pallas_call | solution.py:557
  162.9 1.0 copy-done.1
  163.9 1.4 copy-done.13
  165.3 27.0 %attend_back.3 = (f32[16,768]{1,0:T(8,128)S(1)}, bf16[1024,768]{1,0:T(8,128)(2,1)S(1)}, bf16[3072,768]{1,0:T(8,128)(2,1)}, bf16[3072,768]{1,0:T(8,128)(2,1)}, bf16[768,768]{1,0:T(8,128)(2,1)S(1)}) custom-call(s32[4]{0:T(128)S(1)} %add.171.qbits, s32[6]{0:T(128)S(1)} %add.172.kbits, ...), custom_call_target="tpu_custom_call", output_to_operand_aliasing={{0}: (16, {})} | custom-call | flops 35999997952 | bytes 8388608 | tf_op jit(solution)/shard_map/attend_back/pallas_call | solution.py:286
  192.5 39.0 %collective-permute-start.4 = (bf16[384,768]{1,0:T(8,128)(2,1)S(1)}, bf16[384,768]{1,0:T(8,128)(2,1)S(1)}, u32[]{:S(2)}, u32[]{:S(2)}) collective-permute-start(bf16[384,768]{1,0:T(8,128)(2,1)S(1)} %get-tuple-element.186.refs_4_), channel_id=1, source_target_pairs={{0,1},{1,0},{2,3},{3,2},{4,5},{5,4},{6,7},{7,6},{8,9},{9,8},{10,11... | collective-permute-start | bytes 1769480 | tf_op jit(solution)/shard_map/ppermute | solution.py:468
  231.5 27.0 %attend_back.4 = (f32[16,768]{1,0:T(8,128)S(1)}, bf16[1024,768]{1,0:T(8,128)(2,1)S(1)}, bf16[3072,768]{1,0:T(8,128)(2,1)}, bf16[3072,768]{1,0:T(8,128)(2,1)}, bf16[768,768]{1,0:T(8,128)(2,1)S(1)}) custom-call(s32[4]{0:T(128)S(1)} %add.171.qbits, s32[6]{0:T(128)S(1)} %add.172.kbits, ...), custom_call_target="tpu_custom_call", output_to_operand_aliasing={{0}: (16, {}), {1}: (17, {}), {2}: (18, {}), {3}: (19, {})} | custom-call | flops 35999997952 | bytes 8388608 | tf_op jit(solution)/shard_map/attend_back/pallas_call | solution.py:286
  258.5 1.0 constant_dynamic-slice_fusion.1
  259.5 11.6 %collective-permute-start.8 = (bf16[384,768]{1,0:T(8,128)(2,1)}, bf16[384,768]{1,0:T(8,128)(2,1)}, u32[]{:S(2)}, u32[]{:S(2)}) collective-permute-start(bf16[384,768]{1,0:T(8,128)(2,1)} %get-tuple-element.184.refs_8_), channel_id=1, source_target_pairs={{0,1},{1,0},{2,3},{3,2},{4,5},{5,4},{6,7},{7,6},{8,9},{9,8},{10,11... | collective-permute-start | bytes 1769480 | tf_op jit(solution)/shard_map/ppermute | solution.py:468
  271.2 0.8 constant_dynamic-slice_fusion.3
  272.1 0.8 copy-done.6
  272.9 26.9 %attend_back.5 = (f32[16,768]{1,0:T(8,128)S(1)}, bf16[1024,768]{1,0:T(8,128)(2,1)S(1)}, bf16[3072,768]{1,0:T(8,128)(2,1)}, bf16[3072,768]{1,0:T(8,128)(2,1)}, bf16[768,768]{1,0:T(8,128)(2,1)S(1)}) custom-call(s32[4]{0:T(128)S(1)} %copy-done.10, s32[6]{0:T(128)S(1)} %copy-done.12, ...), custom_call_target="tpu_custom_call", output_to_operand_aliasing={{0}: (16, {}), {1}: (17, {}), {2}: (18, {}), {3}: (19, {})} | custom-call | flops 35999997952 | bytes 8388608 | tf_op jit(solution)/shard_map/attend_back/pallas_call | solution.py:286
  299.9 11.7 %collective-permute-start.9 = (bf16[384,768]{1,0:T(8,128)(2,1)S(1)}, bf16[384,768]{1,0:T(8,128)(2,1)}, u32[]{:S(2)}, u32[]{:S(2)}) collective-permute-start(bf16[384,768]{1,0:T(8,128)(2,1)S(1)} %constant_dynamic-slice_fusion), channel_id=1, source_target_pairs={{0,1},{1,0},{2,3},{3,2},{4,5},{5,4},{6,7},{7,6},{8,9},{9,8},{10,11... | collective-permute-start | bytes 1769480 | tf_op jit(solution)/shard_map/ppermute | solution.py:468
  311.6 20.1 %collective-permute-start.7 = (bf16[96,768]{1,0:T(8,128)(2,1)}, bf16[96,768]{1,0:T(8,128)(2,1)S(1)}, u32[]{:S(2)}, u32[]{:S(2)}) collective-permute-start(bf16[96,768]{1,0:T(8,128)(2,1)} %get-tuple-element.196.refs_6_), channel_id=1, source_target_pairs={{0,6},{1,7},{2,4},{3,5},{4,2},{5,3},{6,0},{7,1},{8,14},{9,15},{10,... | collective-permute-start | bytes 442376 | tf_op jit(solution)/shard_map/ppermute | solution.py:468
  332.4 5.9 %back_product.3 = bf16[1024,768]{1,0:T(8,128)(2,1)} custom-call(bf16[3072,768]{1,0:T(8,128)(2,1)} %get-tuple-element.146.dk, bf16[3072,768]{1,0:T(8,128)(2,1)} %get-tuple-element.138.dv, bf16[768,768]{1,0:T(8,128)(2,1)} %w_key.11, bf16[768,768]{1,0:T(8,128)(2,1)} %w_value.11), custom_call_target="tpu_custom_call" | custom-call | flops 2415919104 | bytes 7864320 | tf_op jit(solution)/shard_map/back_product/pallas_call | solution.py:448
  339.1 2.2 collective-permute-done.5
  341.3 1.2 add_convert_fusion.1
  342.6 1.2 add_convert_fusion
  343.9 1.0 fusion
  344.9 2.3 reduce-scatter.2.cloned.1.call-done
  347.3 1.4 collective-permute-start.12
  348.7 2.1 collective-permute-start.13
  350.8 1.1 add_convert_fusion.4
  351.9 1.8 collective-permute-start.18
  353.7 6.2 %back_product.4 = bf16[1024,768]{1,0:T(8,128)(2,1)} custom-call(bf16[3072,768]{1,0:T(8,128)(2,1)} %get-tuple-element.146.dk, bf16[3072,768]{1,0:T(8,128)(2,1)} %get-tuple-element.138.dv, bf16[768,768]{1,0:T(8,128)(2,1)} %w_key.11, bf16[768,768]{1,0:T(8,128)(2,1)} %w_value.11), custom_call_target="tpu_custom_call" | custom-call | flops 2415919104 | bytes 7864320 | tf_op jit(solution)/shard_map/back_product/pallas_call | solution.py:448
  359.9 5.3 %collective-permute-done.13 = bf16[104,1536]{1,0:T(8,128)(2,1)} collective-permute-done((bf16[104,1536]{1,0:T(8,128)(2,1)}, bf16[104,1536]{1,0:T(8,128)(2,1)}, u32[]{:S(2)}, u32[]{:S(2)}) %collective-permute-start.13) | collective-permute-done | bytes 319520 | tf_op jit(solution)/shard_map/ppermute | solution.py:468
  365.2 0.8 add_convert_fusion.7
  366.6 1.1 add_convert_fusion.3
  367.9 0.8 collective-permute-start.15
  368.6 3.6 collective-permute-start.14
  372.2 9.5 %back_product.5 = bf16[1024,768]{1,0:T(8,128)(2,1)} custom-call(bf16[3072,768]{1,0:T(8,128)(2,1)} %get-tuple-element.146.dk, bf16[3072,768]{1,0:T(8,128)(2,1)} %get-tuple-element.138.dv, bf16[768,768]{1,0:T(8,128)(2,1)} %w_key.11, bf16[768,768]{1,0:T(8,128)(2,1)} %w_value.11, bf16[1024,768]{1,0:T(8,128)(2,1)} %copy-done, bf16[768,768]{1,0:T(8,128)(2,1)} %refs_1_.3, ...), custom_call_target="tpu_custom_call" | custom-call | flops 3623878656 | bytes 7864320 | tf_op jit(solution)/shard_map/back_product/pallas_call | solution.py:448
  381.8 3.8 collective-permute-done.14
  385.7 2.0 collective-permute-start.21
  387.7 3.4 collective-permute-start.20
  391.2 6.9 %collective-permute-done.21 = bf16[24,2304]{1,0:T(8,128)(2,1)S(1)} collective-permute-done((bf16[24,2304]{1,0:T(8,128)(2,1)S(1)}, bf16[24,2304]{1,0:T(8,128)(2,1)S(1)}, u32[]{:S(2)}, u32[]{:S(2)}) %collective-permute-start.21) | collective-permute-done | bytes 110624 | tf_op jit(solution)/shard_map/ppermute | solution.py:468
  398.0 7.5 %collective-permute-done.19 = bf16[24,2304]{1,0:T(8,128)(2,1)S(1)} collective-permute-done((bf16[24,2304]{1,0:T(8,128)(2,1)S(1)}, bf16[24,2304]{1,0:T(8,128)(2,1)S(1)}, u32[]{:S(2)}, u32[]{:S(2)}) %collective-permute-start.19) | collective-permute-done | bytes 110624 | tf_op jit(solution)/shard_map/ppermute | solution.py:468
  405.7 2.6 collective-permute-start.22
  408.3 1.1 collective-permute-start.24
  409.4 4.5 collective-permute-done.22
  414.4 1.5 collective-permute-start.25
  415.9 2.4 collective-permute-start.23
  418.3 18.0 %collective-permute-done.25 = bf16[192,1152]{1,0:T(8,128)(2,1)S(1)} collective-permute-done((bf16[192,1152]{1,0:T(8,128)(2,1)S(1)}, bf16[192,1152]{1,0:T(8,128)(2,1)S(1)}, u32[]{:S(2)}, u32[]{:S(2)}) %collective-permute-start.25) | collective-permute-done | bytes 442400 | tf_op jit(solution)/shard_map/ppermute | solution.py:468
  436.7 1.3 collective-permute-done.23
  438.1 1.3 pad_maximum_fusion.1
  439.4 0.8 add_convert_fusion.6
  441.5 1.3 reshape.98
  442.8 1.5 convert_reduce_fusion
  445.2 3.0 split.1
  448.2 10.8 %all-gather.2.cloned.1.call-done.from_down.from_up.from_out = bf16[768,6912]{1,0:T(8,128)(2,1)} async-done(((bf16[24,6912]{1,0:T(8,128)(2,1)}), bf16[768,6912]{1,0:T(8,128)(2,1)}) %all-gather.2.cloned.1.call-update) | async-done | bytes 10616848 | tf_op jit(solution)/shard_map/all_gather | solution.py:704
  459.0 12.3 %place.1 = (f32[3072,768]{1,0:T(8,128)}, f32[768,3072]{1,0:T(8,128)}, f32[768,768]{1,0:T(8,128)}) custom-call(bf16[768,6912]{1,0:T(8,128)(2,1)} %all-gather.2.cloned.1.call-done.from_down.from_up.from_out, bf16[768,6912]{1,0:T(8,128)(2,1)} %all-gather.2.cloned.1.call-done.from_down.from_up.from_out, ...), custom_call_target="tpu_custom_call" | custom-call | bytes 28311552 | tf_op jit(solution)/shard_map/place/pallas_call | solution.py:581
  (120 shorter events, 7.2 us)
Async XLA Ops:
  7.2 340.0 %reduce-scatter.2.cloned.1.call-start = ((), (), s32[]{:S(2)}) async-start(), calls=%async_computation.1 | async-start | bytes 10948608 | tf_op jit(solution)/shard_map/reduce_scatter | solution.py:666
  8.0 17.3 %collective-permute-start.1 = (s32[1024]{0:T(1024)S(1)}, s32[1024]{0:T(1024)S(1)}, u32[]{:S(2)}, u32[]{:S(2)}) collective-permute-start(s32[1024]{0:T(1024)S(1)} %get-tuple-element.178), channel_id=1, source_target_pairs={{1,2},{2,1},{5,6},{6,5},{9,10},{10,9},{13,14},{14,13},{17,18},{18,... | collective-permute-start | bytes 12296 | tf_op jit(solution)/shard_map/ppermute | solution.py:641
  8.7 16.6 %collective-permute-start = (s32[1024]{0:T(1024)S(1)}, s32[1024]{0:T(1024)S(1)}, u32[]{:S(2)}, u32[]{:S(2)}) collective-permute-start(s32[1024]{0:T(1024)S(1)} %get-tuple-element.178), channel_id=1, source_target_pairs={{0,1},{1,0},{2,3},{3,2},{4,5},{5,4},{6,7},{7,6},{8,9},{9,8},{10,11... | collective-permute-start | bytes 12296 | tf_op jit(solution)/shard_map/ppermute | solution.py:640
  13.1 22.0 %collective-permute-start.3 = (bf16[1024,768]{1,0:T(8,128)(2,1)}, bf16[1024,768]{1,0:T(8,128)(2,1)S(1)}, u32[]{:S(2)}, u32[]{:S(2)}) collective-permute-start(bf16[1024,768]{1,0:T(8,128)(2,1)} %own_in.5), channel_id=1, source_target_pairs={{1,2},{2,1},{5,6},{6,5},{9,10},{10,9},{13,14},{14,13},{17,18},{18,... | collective-permute-start | bytes 4718600 | tf_op jit(solution)/shard_map/ppermute | solution.py:641
  13.8 14.5 %collective-permute-start.2 = (bf16[1024,768]{1,0:T(8,128)(2,1)}, bf16[1024,768]{1,0:T(8,128)(2,1)S(1)}, u32[]{:S(2)}, u32[]{:S(2)}) collective-permute-start(bf16[1024,768]{1,0:T(8,128)(2,1)} %own_in.5), channel_id=1, source_target_pairs={{0,1},{1,0},{2,3},{3,2},{4,5},{5,4},{6,7},{7,6},{8,9},{9,8},{10,11... | collective-permute-start | bytes 4718600 | tf_op jit(solution)/shard_map/ppermute | solution.py:640
  25.3 206.2 %copy-start.9 = (s32[4]{0:T(128)}, s32[4]{0:T(128)S(1)}, u32[]{:S(2)}) copy-start(s32[4]{0:T(128)S(1)} %add.171.qbits) | copy-start | bytes 52
  25.5 206.0 %copy-start.11 = (s32[6]{0:T(128)}, s32[6]{0:T(128)S(1)}, u32[]{:S(2)}) copy-start(s32[6]{0:T(128)S(1)} %add.172.kbits) | copy-start | bytes 76
  28.3 1.1 copy-start.24
  35.0 1.1 copy-start.23
  162.8 1.1 copy-start.1
  162.8 1.1 copy-start.4
  162.8 296.2 %all-gather.2.cloned.1.call-start = ((), (), s32[]{:S(2)}) async-start(), calls=%async_computation.2 | async-start | bytes 10948608 | tf_op jit(solution)/shard_map/all_gather | solution.py:704
  163.9 1.4 copy-start.13
  192.5 78.6 %collective-permute-start.4 = (bf16[384,768]{1,0:T(8,128)(2,1)S(1)}, bf16[384,768]{1,0:T(8,128)(2,1)S(1)}, u32[]{:S(2)}, u32[]{:S(2)}) collective-permute-start(bf16[384,768]{1,0:T(8,128)(2,1)S(1)} %get-tuple-element.186.refs_4_), channel_id=1, source_target_pairs={{0,1},{1,0},{2,3},{3,2},{4,5},{5,4},{6,7},{7,6},{8,9},{9,8},{10,11... | collective-permute-start | bytes 1769480 | tf_op jit(solution)/shard_map/ppermute | solution.py:468
  258.5 13.6 %copy-start.5 = (f32[16,768]{1,0:T(8,128)}, f32[16,768]{1,0:T(8,128)S(1)}, u32[]{:S(2)}) copy-start(f32[16,768]{1,0:T(8,128)S(1)} %get-tuple-element.122.sums_in) | copy-start | bytes 147460
  259.5 12.6 %copy-start.10 = (s32[4]{0:T(128)S(1)}, s32[4]{0:T(128)}, u32[]{:S(2)}) copy-start(s32[4]{0:T(128)} %copy-done.9) | copy-start | bytes 52
  259.5 12.6 %copy-start.12 = (s32[6]{0:T(128)S(1)}, s32[6]{0:T(128)}, u32[]{:S(2)}) copy-start(s32[6]{0:T(128)} %copy-done.11) | copy-start | bytes 76
  259.5 81.8 %collective-permute-start.8 = (bf16[384,768]{1,0:T(8,128)(2,1)}, bf16[384,768]{1,0:T(8,128)(2,1)}, u32[]{:S(2)}, u32[]{:S(2)}) collective-permute-start(bf16[384,768]{1,0:T(8,128)(2,1)} %get-tuple-element.184.refs_8_), channel_id=1, source_target_pairs={{0,1},{1,0},{2,3},{3,2},{4,5},{5,4},{6,7},{7,6},{8,9},{9,8},{10,11... | collective-permute-start | bytes 1769480 | tf_op jit(solution)/shard_map/ppermute | solution.py:468
  272.1 27.8 %copy-start.2 = (bf16[96,768]{1,0:T(8,128)(2,1)}, bf16[96,768]{1,0:T(8,128)(2,1)S(1)}, u32[]{:S(2)}) copy-start(bf16[96,768]{1,0:T(8,128)(2,1)S(1)} %get-tuple-element.199.refs_3_) | copy-start | bytes 442372
  272.1 0.8 copy-start.6
  299.8 32.6 %copy-start.7 = (f32[16,768]{1,0:T(8,128)}, f32[16,768]{1,0:T(8,128)S(1)}, u32[]{:S(2)}) copy-start(f32[16,768]{1,0:T(8,128)S(1)} %get-tuple-element.136) | copy-start | bytes 147460
  299.9 38.5 %copy-start = (bf16[1024,768]{1,0:T(8,128)(2,1)}, bf16[1024,768]{1,0:T(8,128)(2,1)S(1)}, u32[]{:S(2)}) copy-start(bf16[1024,768]{1,0:T(8,128)(2,1)S(1)} %get-tuple-element.150.refs_0_) | copy-start | bytes 4718596
  299.9 42.6 %collective-permute-start.9 = (bf16[384,768]{1,0:T(8,128)(2,1)S(1)}, bf16[384,768]{1,0:T(8,128)(2,1)}, u32[]{:S(2)}, u32[]{:S(2)}) collective-permute-start(bf16[384,768]{1,0:T(8,128)(2,1)S(1)} %constant_dynamic-slice_fusion), channel_id=1, source_target_pairs={{0,1},{1,0},{2,3},{3,2},{4,5},{5,4},{6,7},{7,6},{8,9},{9,8},{10,11... | collective-permute-start | bytes 1769480 | tf_op jit(solution)/shard_map/ppermute | solution.py:468
  311.6 27.3 %collective-permute-start.7 = (bf16[96,768]{1,0:T(8,128)(2,1)}, bf16[96,768]{1,0:T(8,128)(2,1)S(1)}, u32[]{:S(2)}, u32[]{:S(2)}) collective-permute-start(bf16[96,768]{1,0:T(8,128)(2,1)} %get-tuple-element.196.refs_6_), channel_id=1, source_target_pairs={{0,6},{1,7},{2,4},{3,5},{4,2},{5,3},{6,0},{7,1},{8,14},{9,15},{10,... | collective-permute-start | bytes 442376 | tf_op jit(solution)/shard_map/ppermute | solution.py:468
  331.8 7.3 %collective-permute-start.6 = (bf16[96,768]{1,0:T(8,128)(2,1)}, bf16[96,768]{1,0:T(8,128)(2,1)}, u32[]{:S(2)}, u32[]{:S(2)}) collective-permute-start(bf16[96,768]{1,0:T(8,128)(2,1)} %get-tuple-element.197.refs_5_), channel_id=1, source_target_pairs={{0,4},{1,5},{2,6},{3,7},{4,0},{5,1},{6,2},{7,3},{8,12},{9,13},{10,... | collective-permute-start | bytes 442376 | tf_op jit(solution)/shard_map/ppermute | solution.py:468
  331.8 9.5 %collective-permute-start.5 = (bf16[96,768]{1,0:T(8,128)(2,1)}, bf16[96,768]{1,0:T(8,128)(2,1)}, u32[]{:S(2)}, u32[]{:S(2)}) collective-permute-start(bf16[96,768]{1,0:T(8,128)(2,1)} %get-tuple-element.198.refs_4_), channel_id=1, source_target_pairs={{0,2},{1,3},{2,0},{3,1},{4,6},{5,7},{6,4},{7,5},{8,10},{9,11},{10,... | collective-permute-start | bytes 442376 | tf_op jit(solution)/shard_map/ppermute | solution.py:468
  338.3 4.2 copy-start.8
  338.9 4.9 %copy-start.19 = (bf16[96,768]{1,0:T(8,128)(2,1)}, bf16[96,768]{1,0:T(8,128)(2,1)S(1)}, u32[]{:S(2)}) copy-start(bf16[96,768]{1,0:T(8,128)(2,1)S(1)} %collective-permute-done.7) | copy-start | bytes 442372
  338.9 3.6 collective-permute-start.10
  342.6 1.3 copy-start.20
  343.9 6.9 %copy-start.3 = (bf16[96,768]{1,0:T(8,128)(2,1)S(1)}, bf16[96,768]{1,0:T(8,128)(2,1)}, u32[]{:S(2)}) copy-start(bf16[96,768]{1,0:T(8,128)(2,1)} %copy-done.2) | copy-start | bytes 442372
  343.9 8.0 %copy-start.14 = (bf16[1024,768]{1,0:T(8,128)(2,1)S(1)}, bf16[1024,768]{1,0:T(8,128)(2,1)}, u32[]{:S(2)}) copy-start(bf16[1024,768]{1,0:T(8,128)(2,1)} %back_product.3) | copy-start | bytes 4718596
  347.2 12.7 %collective-permute-start.11 = (bf16[104,1536]{1,0:T(8,128)(2,1)}, bf16[104,1536]{1,0:T(8,128)(2,1)S(1)}, u32[]{:S(2)}, u32[]{:S(2)}) collective-permute-start(bf16[104,1536]{1,0:T(8,128)(2,1)} %get-tuple-element.141), channel_id=1, source_target_pairs={{0,2},{1,3},{2,0},{3,1},{4,6},{5,7},{6,4},{7,5},{8,10},{9,11},{10,... | collective-permute-start | bytes 958472 | tf_op jit(solution)/shard_map/ppermute | solution.py:468
  347.3 12.6 %collective-permute-start.12 = (bf16[104,1536]{1,0:T(8,128)(2,1)}, bf16[104,1536]{1,0:T(8,128)(2,1)S(1)}, u32[]{:S(2)}, u32[]{:S(2)}) collective-permute-start(bf16[104,1536]{1,0:T(8,128)(2,1)} %get-tuple-element.142), channel_id=1, source_target_pairs={{0,4},{1,5},{2,6},{3,7},{4,0},{5,1},{6,2},{7,3},{8,12},{9,13},{10,... | collective-permute-start | bytes 958472 | tf_op jit(solution)/shard_map/ppermute | solution.py:468
  348.7 16.5 %collective-permute-start.13 = (bf16[104,1536]{1,0:T(8,128)(2,1)}, bf16[104,1536]{1,0:T(8,128)(2,1)}, u32[]{:S(2)}, u32[]{:S(2)}) collective-permute-start(bf16[104,1536]{1,0:T(8,128)(2,1)} %get-tuple-element.143), channel_id=1, source_target_pairs={{0,6},{1,7},{2,4},{3,5},{4,2},{5,3},{6,0},{7,1},{8,14},{9,15},{10,... | collective-permute-start | bytes 958472 | tf_op jit(solution)/shard_map/ppermute | solution.py:468
  351.9 13.3 %copy-start.21 = (bf16[8,768]{1,0:T(8,128)(2,1)S(1)}, bf16[8,768]{1,0:T(8,128)(2,1)}, u32[]{:S(2)}) copy-start(bf16[8,768]{1,0:T(8,128)(2,1)} %copy-done.20) | copy-start | bytes 36868
  351.9 20.3 %collective-permute-start.18 = (bf16[1024,768]{1,0:T(8,128)(2,1)S(1)}, bf16[1024,768]{1,0:T(8,128)(2,1)}, u32[]{:S(2)}, u32[]{:S(2)}) collective-permute-start(bf16[1024,768]{1,0:T(8,128)(2,1)S(1)} %copy-done.14), channel_id=1, source_target_pairs={{1,2},{2,1},{5,6},{6,5},{9,10},{10,9},{13,14},{14,13},{17,18},{18,... | collective-permute-start | bytes 4718600 | tf_op jit(solution)/shard_map/ppermute | solution.py:641
  365.2 7.0 %collective-permute-start.17 = (bf16[1024,768]{1,0:T(8,128)(2,1)}, bf16[1024,768]{1,0:T(8,128)(2,1)}, u32[]{:S(2)}, u32[]{:S(2)}) collective-permute-start(bf16[1024,768]{1,0:T(8,128)(2,1)} %back_product.4), channel_id=1, source_target_pairs={{0,1},{1,0},{2,3},{3,2},{4,5},{5,4},{6,7},{7,6},{8,9},{9,8},{10,11... | collective-permute-start | bytes 4718600 | tf_op jit(solution)/shard_map/ppermute | solution.py:640
  366.0 0.6 copy-start.15
  367.8 14.0 %collective-permute-start.16 = (bf16[32,2304]{1,0:T(8,128)(2,1)S(1)}, bf16[32,2304]{1,0:T(8,128)(2,1)S(1)}, u32[]{:S(2)}, u32[]{:S(2)}) collective-permute-start(bf16[32,2304]{1,0:T(8,128)(2,1)S(1)} %get-tuple-element.213), channel_id=1, source_target_pairs={{0,24},{1,25},{2,26},{3,27},{4,28},{5,29},{6,30},{7,31},{8,16},{9,... | collective-permute-start | bytes 442376 | tf_op jit(solution)/shard_map/ppermute | solution.py:468
  367.9 13.9 %collective-permute-start.15 = (bf16[32,2304]{1,0:T(8,128)(2,1)S(1)}, bf16[32,2304]{1,0:T(8,128)(2,1)S(1)}, u32[]{:S(2)}, u32[]{:S(2)}) collective-permute-start(bf16[32,2304]{1,0:T(8,128)(2,1)S(1)} %get-tuple-element.214), channel_id=1, source_target_pairs={{0,8},{1,9},{2,10},{3,11},{4,12},{5,13},{6,14},{7,15},{8,0},{9,1},... | collective-permute-start | bytes 442376 | tf_op jit(solution)/shard_map/ppermute | solution.py:468
  368.6 17.0 %collective-permute-start.14 = (bf16[32,2304]{1,0:T(8,128)(2,1)S(1)}, bf16[32,2304]{1,0:T(8,128)(2,1)S(1)}, u32[]{:S(2)}, u32[]{:S(2)}) collective-permute-start(bf16[32,2304]{1,0:T(8,128)(2,1)S(1)} %get-tuple-element.215), channel_id=1, source_target_pairs={{0,16},{1,17},{2,18},{3,19},{4,20},{5,21},{6,22},{7,23},{8,24},{9,... | collective-permute-start | bytes 442376 | tf_op jit(solution)/shard_map/ppermute | solution.py:468
  381.7 23.8 %copy-start.16 = (bf16[32,2304]{1,0:T(8,128)(2,1)}, bf16[32,2304]{1,0:T(8,128)(2,1)S(1)}, u32[]{:S(2)}) copy-start(bf16[32,2304]{1,0:T(8,128)(2,1)S(1)} %collective-permute-done.16) | copy-start | bytes 442372
  381.8 23.8 %copy-start.17 = (bf16[32,2304]{1,0:T(8,128)(2,1)}, bf16[32,2304]{1,0:T(8,128)(2,1)S(1)}, u32[]{:S(2)}) copy-start(bf16[32,2304]{1,0:T(8,128)(2,1)S(1)} %collective-permute-done.15) | copy-start | bytes 442372
  385.6 20.1 %copy-start.18 = (bf16[32,2304]{1,0:T(8,128)(2,1)}, bf16[32,2304]{1,0:T(8,128)(2,1)S(1)}, u32[]{:S(2)}) copy-start(bf16[32,2304]{1,0:T(8,128)(2,1)S(1)} %collective-permute-done.14) | copy-start | bytes 442372
  385.7 12.4 %collective-permute-start.21 = (bf16[24,2304]{1,0:T(8,128)(2,1)S(1)}, bf16[24,2304]{1,0:T(8,128)(2,1)S(1)}, u32[]{:S(2)}, u32[]{:S(2)}) collective-permute-start(bf16[24,2304]{1,0:T(8,128)(2,1)S(1)} %add_convert_fusion.5), channel_id=1, source_target_pairs={{0,8},{1,9},{2,10},{3,11},{4,12},{5,13},{6,14},{7,15},{8,0},{9,1},... | collective-permute-start | bytes 331784 | tf_op jit(solution)/shard_map/ppermute | solution.py:468
  387.7 10.3 %collective-permute-start.20 = (bf16[24,2304]{1,0:T(8,128)(2,1)S(1)}, bf16[24,2304]{1,0:T(8,128)(2,1)S(1)}, u32[]{:S(2)}, u32[]{:S(2)}) collective-permute-start(bf16[24,2304]{1,0:T(8,128)(2,1)S(1)} %add_convert_fusion.5), channel_id=1, source_target_pairs={{0,16},{1,17},{2,18},{3,19},{4,20},{5,21},{6,22},{7,23},{8,24},{9,... | collective-permute-start | bytes 331784 | tf_op jit(solution)/shard_map/ppermute | solution.py:468
  391.2 14.4 %collective-permute-start.19 = (bf16[24,2304]{1,0:T(8,128)(2,1)S(1)}, bf16[24,2304]{1,0:T(8,128)(2,1)S(1)}, u32[]{:S(2)}, u32[]{:S(2)}) collective-permute-start(bf16[24,2304]{1,0:T(8,128)(2,1)S(1)} %add_convert_fusion.5), channel_id=1, source_target_pairs={{0,24},{1,25},{2,26},{3,27},{4,28},{5,29},{6,30},{7,31},{8,16},{9,... | collective-permute-start | bytes 331784 | tf_op jit(solution)/shard_map/ppermute | solution.py:468
  405.7 8.2 %collective-permute-start.22 = (bf16[96,1152]{1,0:T(8,128)(2,1)S(1)}, bf16[96,1152]{1,0:T(8,128)(2,1)S(1)}, u32[]{:S(2)}, u32[]{:S(2)}) collective-permute-start(bf16[96,1152]{1,0:T(8,128)(2,1)S(1)} %get-tuple-element.202), channel_id=1, source_target_pairs={{0,2},{1,3},{2,0},{3,1},{4,6},{5,7},{6,4},{7,5},{8,10},{9,11},{10,... | collective-permute-start | bytes 663560 | tf_op jit(solution)/shard_map/ppermute | solution.py:468
  408.3 6.0 %collective-permute-start.24 = (bf16[96,1152]{1,0:T(8,128)(2,1)S(1)}, bf16[96,1152]{1,0:T(8,128)(2,1)S(1)}, u32[]{:S(2)}, u32[]{:S(2)}) collective-permute-start(bf16[96,1152]{1,0:T(8,128)(2,1)S(1)} %get-tuple-element.203), channel_id=1, source_target_pairs={{0,4},{1,5},{2,6},{3,7},{4,0},{5,1},{6,2},{7,3},{8,12},{9,13},{10,... | collective-permute-start | bytes 663560 | tf_op jit(solution)/shard_map/ppermute | solution.py:468
  414.4 21.9 %collective-permute-start.25 = (bf16[192,1152]{1,0:T(8,128)(2,1)S(1)}, bf16[192,1152]{1,0:T(8,128)(2,1)S(1)}, u32[]{:S(2)}, u32[]{:S(2)}) collective-permute-start(bf16[192,1152]{1,0:T(8,128)(2,1)S(1)} %pad_maximum_fusion.5), channel_id=1, source_target_pairs={{0,2},{1,3},{2,0},{3,1},{4,6},{5,7},{6,4},{7,5},{8,10},{9,11},{10,... | collective-permute-start | bytes 1327112 | tf_op jit(solution)/shard_map/ppermute | solution.py:468
  415.9 22.0 %collective-permute-start.23 = (bf16[192,1152]{1,0:T(8,128)(2,1)S(1)}, bf16[192,1152]{1,0:T(8,128)(2,1)S(1)}, u32[]{:S(2)}, u32[]{:S(2)}) collective-permute-start(bf16[192,1152]{1,0:T(8,128)(2,1)S(1)} %pad_maximum_fusion.4), channel_id=1, source_target_pairs={{0,4},{1,5},{2,6},{3,7},{4,0},{5,1},{6,2},{7,3},{8,12},{9,13},{10,... | collective-permute-start | bytes 1327112 | tf_op jit(solution)/shard_map/ppermute | solution.py:468
  439.4 4.8 %collective-permute-start.26 = (bf16[384,2304]{1,0:T(8,128)(2,1)}, bf16[384,2304]{1,0:T(8,128)(2,1)S(1)}, u32[]{:S(2)}, u32[]{:S(2)}) collective-permute-start(bf16[384,2304]{1,0:T(8,128)(2,1)} %pad_maximum_fusion.1), channel_id=1, source_target_pairs={{0,1},{1,0},{2,3},{3,2},{4,5},{5,4},{6,7},{7,6},{8,9},{9,8},{10,11... | collective-permute-start | bytes 5308424 | tf_op jit(solution)/shard_map/ppermute | solution.py:468
  440.3 0.6 copy-start.22
Sparse Core Ops, SparseCore 0:
  162.9 184.1 reduce-scatter.1
  350.1 108.9 all-gather.1
